TPU v7x, 128 devices: a whole 4x4x4 slice. The times are simulated.
128 devices in a mesh: lat: 4 (over y), patch: 32 (over x, z, core).
Axes of the slice: x: 4, y: 4, z: 4, core: 2. Of those that a mesh axis runs over, the one named last changes fastest.
Arguments:
- coarse: bfloat16 [8192, 64, 128], P(('lat', 'patch')), may hold values from -6 to 6
- slot_owner: int32 [128, 112, 1], replicated, may hold values from 0 to 127; in each aligned block of 112 rows (0 to 111, 112 to 223, ..., all dimensions but the last counted through in order) at most 2 rows name the same one
- slot_block: int32 [128, 112], replicated, may hold values from 0 to 63
- interp: bfloat16 [128, 56], replicated, may hold values from -0.5 to 0.5
- lift: bfloat16 [128, 64], replicated, may hold values from -0.75 to 0.75
- conv_weights: bfloat16 [4, 9, 128, 128], replicated, may hold values from -0.1875 to 0.1875
- gains: float32 [4, 128], replicated, may hold values from 0.1 to 1.9
- fine_noisy: bfloat16 [32, 128, 56, 448], P('patch', None, 'lat'), may hold values from -20 to 20
- out_grad: float32 [32, 128, 56, 448], P('patch', None, 'lat'), may hold values from -6 to 6
Outputs:
- denoised: float32 [32, 128, 56, 448], P('patch', None, 'lat')
- coarse_grad: float32 [8192, 64, 128], P(('lat', 'patch'))
- interp_grad: float32 [128, 56], replicated
- lift_grad: float32 [128, 64], replicated
- conv_grads: float32 [4, 9, 128, 128], replicated
- gain_grads: float32 [4, 128], replicated
Inputs may be any that keep to these rules, and one draw needn't show every extreme that they name: `slot_owner`: among the 112 slots of one tile no owner is named more than 2 times, and in every draw some tile names some owner exactly 2 times; every owner is named somewhere.
All inputs are finite; a program needn't handle non-finite values.
Results may differ from a plain program's by a relative error of at most 0.012.
Values may be sent and summed in bfloat16 or wider, within the bound.
No kernel may reach another device: no remote copies, remote signals or barrier semaphores. Data moves between devices by JAX's collectives and lax.ppermute only.
A program may use at most 192 MiB of HBM per device.

v0:
```python
import math

import jax
import jax.numpy as jnp
from jax import lax
from jax.sharding import PartitionSpec as P

GROUPS = 32


EPSILON = 1e-05


def padded_2(cells, sides, width):
    for axis, dim in sides:
        count = lax.axis_size(axis)
        ends = count - 1
        head = lax.slice_in_dim(cells, 0, width, axis=dim)
        tail = lax.slice_in_dim(cells, cells.shape[dim] - width, cells.shape[dim], axis=dim)
        cells = jnp.concatenate(
            [
                lax.ppermute(tail, axis, [(i, (i + 1) % count) for i in range(ends)]),
                cells,
                lax.ppermute(head, axis, [((i + 1) % count, i) for i in range(ends)]),
            ],
            axis=dim,
        )
    return cells


def bordered(values):
    rows_done = padded_2(values, (("lat", 1),), 1)
    return jnp.pad(rows_done, ((0, 0), (0, 0), (1, 1)))


def global_pair(first_sum, second_sum):
    return lax.psum((first_sum, second_sum), "lat")


def conv_apply(padded, weights):
    out_rows = padded.shape[1] - 2
    out_cols = padded.shape[2] - 2
    summed = jnp.zeros((weights.shape[1], out_rows, out_cols), jnp.float32)
    for offset in range(9):
        row_shift = offset // 3
        col_shift = offset % 3
        window = padded[:, row_shift : row_shift + out_rows, col_shift : col_shift + out_cols]
        summed = summed + jnp.einsum(
            "oc,crw->orw", weights[offset], window, preferred_element_type=jnp.float32
        )
    return summed


def conv_transpose(padded_grad, weights):
    out_rows = padded_grad.shape[1] - 2
    out_cols = padded_grad.shape[2] - 2
    summed = jnp.zeros((weights.shape[2], out_rows, out_cols), jnp.float32)
    for offset in range(9):
        row_shift = 2 - offset // 3
        col_shift = 2 - offset % 3
        window = padded_grad[:, row_shift : row_shift + out_rows, col_shift : col_shift + out_cols]
        summed = summed + jnp.einsum(
            "oc,orw->crw", weights[offset], window, preferred_element_type=jnp.float32
        )
    return summed


def kernel_grad(gradient, padded):
    out_rows = gradient.shape[1]
    out_cols = gradient.shape[2]
    terms = []
    for offset in range(9):
        row_shift = offset // 3
        col_shift = offset % 3
        window = padded[:, row_shift : row_shift + out_rows, col_shift : col_shift + out_cols]
        terms.append(
            jnp.einsum("orw,crw->oc", gradient, window, preferred_element_type=jnp.float32)
        )
    return jnp.stack(terms)


def norm_act(values, gain_row, cell_count):
    grouped = values.reshape(GROUPS, -1)
    group_sum, group_square = global_pair(jnp.sum(grouped, 1), jnp.sum(grouped * grouped, 1))
    group_mean = group_sum / cell_count
    inv_spread = lax.rsqrt(group_square / cell_count - group_mean * group_mean + EPSILON)
    per_group = values.shape[0] // GROUPS
    mean_col = jnp.repeat(group_mean, per_group)[:, None, None]
    spread_col = jnp.repeat(inv_spread, per_group)[:, None, None]
    normed = (values - mean_col) * spread_col
    scaled = normed * gain_row[:, None, None]
    return (normed, spread_col, scaled, (scaled * jax.nn.sigmoid(scaled)).astype(jnp.bfloat16))


def norm_back(grad_act, normed, spread_col, scaled, gain_row, cell_count):
    sigmoid_y = jax.nn.sigmoid(scaled)
    grad_scaled = grad_act * sigmoid_y * (1.0 + scaled * (1.0 - sigmoid_y))
    gain_term = jnp.sum(grad_scaled * normed, axis=(1, 2))
    grad_normed = grad_scaled * gain_row[:, None, None]
    first_sum, second_sum = global_pair(
        jnp.sum(grad_normed.reshape(GROUPS, -1), 1),
        jnp.sum((grad_normed * normed).reshape(GROUPS, -1), 1),
    )
    per_group = grad_normed.shape[0] // GROUPS
    first_col = jnp.repeat(first_sum / cell_count, per_group)[:, None, None]
    second_col = jnp.repeat(second_sum / cell_count, per_group)[:, None, None]
    return (spread_col * (grad_normed - first_col - normed * second_col), gain_term)


def block_forward(values, conv_weights, gains, first_index, cell_count):
    normed_a, spread_a, scaled_a, act_a = norm_act(values, gains[first_index], cell_count)
    padded_a = bordered(act_a)
    conv_a = conv_apply(padded_a, conv_weights[first_index])
    normed_b, spread_b, scaled_b, act_b = norm_act(conv_a, gains[first_index + 1], cell_count)
    padded_b = bordered(act_b)
    conv_b = conv_apply(padded_b, conv_weights[first_index + 1])
    saved = (normed_a, spread_a, scaled_a, padded_a, normed_b, spread_b, scaled_b, padded_b)
    return (values + conv_b, saved)


def block_back(grad_out, saved, conv_weights, gains, first_index, cell_count):
    normed_a, spread_a, scaled_a, padded_a, normed_b, spread_b, scaled_b, padded_b = saved
    grad_b = grad_out.astype(jnp.bfloat16)
    kernel_b = kernel_grad(grad_b, padded_b)
    grad_act_b = conv_transpose(bordered(grad_b), conv_weights[first_index + 1])
    grad_conv, gain_b = norm_back(
        grad_act_b, normed_b, spread_b, scaled_b, gains[first_index + 1], cell_count
    )
    grad_a = grad_conv.astype(jnp.bfloat16)
    kernel_a = kernel_grad(grad_a, padded_a)
    grad_act_a = conv_transpose(bordered(grad_a), conv_weights[first_index])
    grad_input, gain_a = norm_back(
        grad_act_a, normed_a, spread_a, scaled_a, gains[first_index], cell_count
    )
    return (grad_out + grad_input, (kernel_a, kernel_b), (gain_a, gain_b))


def pool_mean(values):
    chans, height, breadth = values.shape
    return values.reshape(chans, height // 2, 2, breadth // 2, 2).mean(axis=(2, 4))


def pool_sum(values):
    chans, height, breadth = values.shape
    return values.reshape(chans, height // 2, 2, breadth // 2, 2).sum(axis=(2, 4))


def widen(values):
    return jnp.repeat(jnp.repeat(values, 2, axis=1), 2, axis=2)


def body(coarse, slot_owner, slot_block, interp, lift, conv_weights, gains, fine_noisy, out_grad):
    devices = lax.axis_size(("lat", "patch"))
    lat_count = lax.axis_size("lat")
    own_index = lax.axis_index(("lat", "patch"))
    owners = slot_owner[:, :, 0]
    slot_count = owners.shape[1]
    capacity = max(2, 2 * slot_count // devices)
    noisy_tile = fine_noisy[0]
    grad_tile = out_grad[0]
    channels, tile_rows, tile_cols = noisy_tile.shape
    coarse_chans = coarse.shape[1]
    block_cells = coarse.shape[2]
    region = interp.shape[1]
    per_row = slot_count // tile_rows
    earlier = (jnp.arange(slot_count)[None, :] < jnp.arange(slot_count)[:, None]).astype(jnp.int32)
    same_owner = (owners[:, :, None] == owners[:, None, :]).astype(jnp.int32)
    position = jnp.sum(same_owner * earlier[None, :, :], axis=2)
    my_owners = lax.dynamic_index_in_dim(owners, own_index, 0, keepdims=False)
    my_position = lax.dynamic_index_in_dim(position, own_index, 0, keepdims=False)
    flat_slot = my_owners * capacity + my_position
    matched = (
        (owners[:, None, :] == own_index)
        & (position[:, None, :] == jnp.arange(capacity)[None, :, None])
    ).astype(jnp.int32)
    send_ids = jnp.sum(matched * slot_block[:, None, :], axis=2).reshape(-1)
    filled = jnp.sum(matched, axis=2).reshape(-1)
    outgoing = jnp.take(coarse, send_ids, axis=0) * filled.astype(jnp.bfloat16)[:, None, None]
    arrived = lax.all_to_all(
        outgoing.reshape(devices, capacity, coarse_chans, block_cells),
        ("lat", "patch"),
        split_axis=0,
        concat_axis=0,
        tiled=True,
    )
    chosen = jnp.take(
        arrived.reshape(devices * capacity, coarse_chans, block_cells), flat_slot, axis=0
    )
    pieces = jnp.einsum("kcb,bq->kcq", chosen, interp, preferred_element_type=jnp.float32).astype(
        jnp.bfloat16
    )
    cond = (
        pieces.reshape(tile_rows, per_row, coarse_chans, region)
        .transpose(2, 0, 1, 3)
        .reshape(coarse_chans, tile_rows, tile_cols)
    )
    hidden = noisy_tile.astype(jnp.float32) + jnp.einsum(
        "oc,crw->orw", lift, cond, preferred_element_type=jnp.float32
    )
    full_count = channels // GROUPS * tile_rows * tile_cols * lat_count
    half_count = full_count // 4
    level_one, saved_one = block_forward(hidden, conv_weights, gains, 0, full_count)
    pooled = pool_mean(level_one)
    level_two, saved_two = block_forward(pooled, conv_weights, gains, 2, half_count)
    denoised = level_one + widen(level_two)
    grad_pooled, kernels_two, gains_two = block_back(
        pool_sum(grad_tile), saved_two, conv_weights, gains, 2, half_count
    )
    grad_level = grad_tile + 0.25 * widen(grad_pooled)
    grad_hidden, kernels_one, gains_one = block_back(
        grad_level, saved_one, conv_weights, gains, 0, full_count
    )
    hidden_grad = grad_hidden.astype(jnp.bfloat16)
    lift_term = jnp.einsum("orw,crw->oc", hidden_grad, cond, preferred_element_type=jnp.float32)
    grad_cond = jnp.einsum(
        "oc,orw->crw", lift, hidden_grad, preferred_element_type=jnp.float32
    ).astype(jnp.bfloat16)
    grad_pieces = (
        grad_cond.reshape(coarse_chans, tile_rows, per_row, region)
        .transpose(1, 2, 0, 3)
        .reshape(slot_count, coarse_chans, region)
    )
    slot_terms = jnp.einsum("kcq,bq->kcb", grad_pieces, interp, preferred_element_type=jnp.float32)
    placed = (
        jnp.zeros((devices * capacity, coarse_chans, block_cells), jnp.float32)
        .at[flat_slot]
        .set(slot_terms)
    )
    block_terms = lax.all_to_all(
        placed.reshape(devices, capacity, coarse_chans, block_cells).astype(jnp.bfloat16),
        ("lat", "patch"),
        split_axis=0,
        concat_axis=0,
        tiled=True,
    ).astype(jnp.float32)
    block_terms = block_terms.reshape(devices * capacity, coarse_chans, block_cells)
    interp_term = jnp.einsum("kcb,kcq->bq", chosen, grad_pieces, preferred_element_type=jnp.float32)
    selector = (
        (send_ids[None, :] == jnp.arange(coarse.shape[0])[:, None]) & (filled[None, :] > 0)
    ).astype(jnp.float32)
    coarse_grad = jnp.dot(
        selector,
        block_terms.reshape(devices * capacity, coarse_chans * block_cells),
        precision=lax.Precision.HIGHEST,
    )
    coarse_grad = coarse_grad.reshape(coarse.shape[0], coarse_chans, block_cells)
    conv_terms = jnp.stack([kernels_one[0], kernels_one[1], kernels_two[0], kernels_two[1]])
    gain_terms = jnp.stack([gains_one[0], gains_one[1], gains_two[0], gains_two[1]])
    conv_total, gain_total, lift_total, interp_total = lax.psum(
        (conv_terms, gain_terms, lift_term, interp_term), ("lat", "patch")
    )
    grad_scale = 1.0 / math.sqrt(tile_rows * tile_cols * devices)
    return (
        denoised[None],
        coarse_grad,
        interp_total * grad_scale,
        lift_total * grad_scale,
        conv_total * grad_scale,
        gain_total * grad_scale,
    )


def solution(mesh):
    placed = (
        P(("lat", "patch"), None, None),
        P(),
        P(),
        P(),
        P(),
        P(),
        P(),
        P("patch", None, "lat", None),
        P("patch", None, "lat", None),
    )
    return jax.shard_map(
        body,
        mesh=mesh,
        in_specs=placed,
        out_specs=(
            P("patch", None, "lat", None),
            P(("lat", "patch"), None, None),
            P(),
            P(),
            P(),
            P(),
        ),
        check_vma=False,
    )
```

profile of v0, /device:TPU:1, one launch (start us, length us, event | category | flops | bytes accessed | tf_op | source)
XLA Modules:
  0.0 723.7 jit_solution(14139567801250391617)
XLA Ops:
  8.1 4.7 select_reduce_fusion
  14.2 3.1 gather_fusion
  17.3 3.9 select_multiply_fusion
  21.2 12.0 %all-to-all-start = ((bf16[128,2,64,128]{3,2,1,0:T(8,128)(2,1)}), bf16[128,2,64,128]{3,2,1,0:T(8,128)(2,1)}, u32[]{:S(2)}, u32[]{:S(2)}) async-start(bf16[128,2,64,128]{3,2,1,0:T(8,128)(2,1)} %select_multiply_fusion), calls=%async_computation | async-start | bytes 8388608 | tf_op jit(solution)/shard_map/all_to_all | solution.py:179
  33.2 3.6 reduce_sum.365
  38.0 3.3 collective-permute-start.8
  47.3 27.6 %collective-permute-done.8 = bf16[128,1,224]{0,2,1:T(8,128)(2,1)S(1)} collective-permute-done((bf16[128,1,224]{0,2,1:T(8,128)(2,1)S(1)}, bf16[128,1,224]{0,2,1:T(8,128)(2,1)S(1)}, u32[]{:S(2)}, u32[]{:S(2)}) %collective-permute-start.8) | collective-permute-done | bytes 57376 | tf_op jit(solution)/shard_map/ppermute | solution.py:22
  75.0 7.1 collective-permute-done.9
  90.4 3.1 gather_fusion.1
  98.3 3.8 reshape.309
  105.3 7.9 %all-reduce.16 = (f32[32]{0:T(128)S(1)}, f32[32]{0:T(128)S(1)}) all-reduce(f32[32]{0:T(128)S(1)} %reduce_sum.276, f32[32]{0:T(128)S(1)} %reduce_sum.270), channel_id=1, replica_groups=mesh['lat'=4,'patch'=32] {'lat'}, use_global_device_ids=true, to_apply=%region_8.9 | all-reduce | flops 64 | bytes 512 | tf_op jit(solution)/shard_map/psum | solution.py:37
  127.6 3.1 fusion.143
  136.7 6.2 fusion.552
  143.3 7.0 all-reduce.15
  169.1 3.0 fusion.117
  175.2 3.1 fusion.21
  178.2 8.5 %bitcast_add_fusion.1 = f32[128,14,448]{0,2,1:T(8,128)} fusion(f32[128,14,448]{0,2,1:T(8,128)S(1)} %get-tuple-element.101, f32[14,448,128]{2,1,0:T(8,128)} %fusion.25, f32[14,448,128]{2,1,0:T(8,128)S(1)} %fusion.101, f32[14,448,128]{2,1,0:T(8,128)S(1)} %fusion.105, f32[14,448,128]{2,1,0:T(8,128)S(1)} %fusion.400, f32[14,448,128]{2,1,0:T(8,128)S(1)} %fusion.109, ...), kind=kOutput, calls=%fused_computation.15 | convolution fusion | flops 212746240 | bytes 33751040 | tf_op jit(solution)/shard_map/oc,crw->orw/dot_general | solution.py:48
  186.7 5.1 reduce_sum.289
  193.6 6.0 all-reduce.14
  201.5 3.4 collective-permute-start.4
  226.2 7.5 %all-reduce.13 = (f32[32]{0:T(128)}, f32[32]{0:T(128)}) all-reduce(f32[32]{0:T(128)} %reduce_sum.364, f32[32]{0:T(128)} %reduce_sum.361), channel_id=1, replica_groups=mesh['lat'=4,'patch'=32] {'lat'}, use_global_device_ids=true, to_apply=%region_27.28 | all-reduce | flops 64 | bytes 512 | tf_op jit(solution)/shard_map/psum | solution.py:37
  239.6 3.9 fusion.279
  248.9 7.5 %all-reduce.12 = (f32[32]{0:T(128)}, f32[32]{0:T(128)}) all-reduce(f32[32]{0:T(128)} %reduce_sum.371, f32[32]{0:T(128)} %reduce_sum.368), channel_id=1, replica_groups=mesh['lat'=4,'patch'=32] {'lat'}, use_global_device_ids=true, to_apply=%region_34.35 | all-reduce | flops 64 | bytes 512 | tf_op jit(solution)/shard_map/psum | solution.py:37
  269.0 4.0 collective-permute-start.10
  291.8 8.1 %all-reduce.11 = (f32[32]{0:T(128)S(1)}, f32[32]{0:T(128)S(1)}) all-reduce(f32[32]{0:T(128)S(1)} %reduce_sum.377, f32[32]{0:T(128)S(1)} %reduce_sum.374), channel_id=1, replica_groups=mesh['lat'=4,'patch'=32] {'lat'}, use_global_device_ids=true, to_apply=%region_40.41 | all-reduce | flops 64 | bytes 512 | tf_op jit(solution)/shard_map/psum | solution.py:37
  321.8 4.8 collective-permute-start.12
  351.1 3.1 fusion.86
  360.2 3.2 fusion.33
  363.4 3.1 fusion.29
  366.6 10.3 %fusion.7 = (f32[128]{0:T(128)S(1)}, f32[128]{0:T(128)S(1)}, f32[128]{0:T(128)S(1)}, f32[128,14,448]{0,2,1:T(8,128)}) fusion(f32[14,448,128]{2,1,0:T(8,128)S(1)} %copy-done.13, f32[128]{0:T(128)S(1)} %copy-done.55, f32[128]{0:T(128)S(1)} %copy-done.63, f32[128]{0:T(128)S(1)} %copy-done.65, bf16[4,9,128,128]{3,2,1,0:T(8,128)(2,1)} %param.14, ...), kind=kOutput, calls=%fused_computation.24 | convolution fusion | flops 225590912 | bytes 33754112 | tf_op jit(solution)/shard_map/oc,orw->crw/dot_general | solution.py:62
  377.3 6.0 all-reduce.10
  383.7 3.7 fusion.6
  390.3 4.0 collective-permute-start.14
  403.6 3.1 fusion.76
  412.6 7.6 %multiply_reduce_fusion.1 = (f32[128]{0:T(128)S(1)}, f32[128]{0:T(128)S(1)}, f32[128]{0:T(128)S(1)}, f32[128,14,448]{0,2,1:T(8,128)}) fusion(f32[128,14,448]{0,2,1:T(8,128)S(1)} %get-tuple-element.101, f32[128]{0:T(128)S(1)} %copy-done.59, f32[128]{0:T(128)S(1)} %copy-done.57, f32[128]{0:T(128)S(1)} %copy-done.61, bf16[4,9,128,128]{3,2,1,0:T(8,128)(2,1)} %param.14, ...), kind=kOutput, calls=%fused_computation.28 | convolution fusion | flops 225590912 | bytes 33754112 | tf_op jit(solution)/shard_map/oc,orw->crw/dot_general | solution.py:62
  420.7 8.6 %all-reduce.9 = (f32[32]{0:T(128)S(1)}, f32[32]{0:T(128)S(1)}) all-reduce(f32[32]{0:T(128)S(1)} %reduce_sum.389, f32[32]{0:T(128)S(1)} %reduce_sum.386), channel_id=1, replica_groups=mesh['lat'=4,'patch'=32] {'lat'}, use_global_device_ids=true, to_apply=%region_52.53 | all-reduce | flops 64 | bytes 512 | tf_op jit(solution)/shard_map/psum | solution.py:37
  429.7 5.0 add_convert_fusion
  443.2 4.3 broadcast_in_dim.110
  447.5 17.0 %scatter_fusion = f32[256,64,128]{2,1,0:T(8,128)} fusion(f32[256,64,128]{2,1,0:T(8,128)} %broadcast_in_dim.110, s32[112]{0:T(128)S(1)} %copy-done.75, f32[112,64,128]{2,1,0:T(8,128)} %fusion.522), kind=kCustom, calls=%fused_computation.2 | custom fusion | bytes 11010496 | tf_op jit(solution)/shard_map/scatter | solution.py:227
  464.5 6.5 convert_element_type.102
  471.0 29.4 %all-to-all-start.1 = ((bf16[128,2,64,128]{3,2,1,0:T(8,128)(2,1)}), bf16[128,2,64,128]{3,2,1,0:T(8,128)(2,1)}, u32[]{:S(2)}, u32[]{:S(2)}) async-start(bf16[128,2,64,128]{3,2,1,0:T(8,128)(2,1)} %bitcast.660), calls=%async_computation.1 | async-start | bytes 8388608 | tf_op jit(solution)/shard_map/all_to_all | solution.py:229
  512.2 3.1 pad_maximum_fusion
  519.5 86.9 %all-reduce.8 = (f32[128,56]{0,1:T(8,128)S(1)}, f32[128,64]{0,1:T(8,128)S(1)}, f32[4,128]{1,0:T(4,128)S(1)}) all-reduce(f32[128,56]{0,1:T(8,128)S(1)} %convolution_bitcast_fusion.21, f32[128,64]{0,1:T(8,128)S(1)} %convolution_bitcast_fusion.20, f32[4,128]{1,0:T(4,128)S(1)} %pad_maximum_fusion.1), channel_id=1, replica_groups=mesh['lat'=4,'patch'=32] {'lat','patch'}, use_global_device_ids=true, to_apply=%region_54.55 | all-reduce | flops 15872 | bytes 126976 | tf_op jit(solution)/shard_map/psum | solution.py:249
  608.2 80.2 %all-reduce.19.cloned.1.call-done = f32[4,9,128,128]{3,2,1,0:T(8,128)} async-done(((f32[4,9,128,128]{3,2,1,0:T(8,128)}), f32[4,9,128,128]{3,2,1,0:T(8,128)}) %all-reduce.19.cloned.1.call-update) | async-done | bytes 2359312 | tf_op jit(solution)/shard_map/psum | solution.py:249
  688.3 3.4 broadcast_multiply_fusion
  691.8 12.3 %copy.54 = bf16[32,8,64,128]{3,1,2,0:T(8,128)(2,1)} copy(bf16[32,8,64,128]{3,2,1,0:T(8,128)(2,1)} %bitcast.237) | data formatting | bytes 8388608
  704.1 6.4 copy.50
  710.5 3.7 fusion.368
  (426 shorter events, 235.9 us)
Async XLA Ops:
  7.2 7.1 copy-start
  21.2 12.0 %copy-start.14 = (f32[1,128,14,448]{1,3,2,0:T(8,128)S(1)}, f32[1,128,14,448]{1,3,2,0:T(8,128)}, u32[]{:S(2)}) copy-start(f32[1,128,14,448]{1,3,2,0:T(8,128)} %param.17) | copy-start | bytes 9633796
  21.2 69.2 %all-to-all-start = ((bf16[128,2,64,128]{3,2,1,0:T(8,128)(2,1)}), bf16[128,2,64,128]{3,2,1,0:T(8,128)(2,1)}, u32[]{:S(2)}, u32[]{:S(2)}) async-start(bf16[128,2,64,128]{3,2,1,0:T(8,128)(2,1)} %select_multiply_fusion), calls=%async_computation | async-start | bytes 8388608 | tf_op jit(solution)/shard_map/all_to_all | solution.py:179
  33.2 11.4 %copy-start.39 = (s32[128,112,1]{0,2,1:T(1,128)S(1)}, s32[128,112,1]{0,2,1:T(1,128)}, u32[]{:S(2)}) copy-start(s32[128,112,1]{0,2,1:T(1,128)} %param.10) | copy-start | bytes 172036
  33.2 13.6 %copy-start.76 = (f32[4,128]{1,0:T(4,128)S(1)}, f32[4,128]{1,0:T(4,128)}, u32[]{:S(2)}) copy-start(f32[4,128]{1,0:T(4,128)} %param.15) | copy-start | bytes 6148
  37.9 48.4 %copy-start.31 = (bf16[128,7,224]{0,2,1:T(8,128)(2,1)}, bf16[128,7,224]{0,2,1:T(8,128)(2,1)S(1)}, u32[]{:S(2)}) copy-start(bf16[128,7,224]{0,2,1:T(8,128)(2,1)S(1)} %convert_element_type.93) | copy-start | bytes 1204228
  38.0 37.0 %collective-permute-start.8 = (bf16[128,1,224]{0,2,1:T(8,128)(2,1)S(1)}, bf16[128,1,224]{0,2,1:T(8,128)(2,1)S(1)}, u32[]{:S(2)}, u32[]{:S(2)}) collective-permute-start(bf16[128,1,224]{0,2,1:T(8,128)(2,1)S(1)} %get-tuple-element.83), channel_id=1, source_target_pairs={{0,32},{32,64},{64,96},{1,33},{33,65},{65,97},{2,34},{34,66},{66,9... | collective-permute-start | bytes 172040 | tf_op jit(solution)/shard_map/ppermute | solution.py:22
  41.3 40.8 %collective-permute-start.9 = (bf16[128,1,224]{0,2,1:T(8,128)(2,1)S(1)}, bf16[128,1,224]{0,2,1:T(8,128)(2,1)S(1)}, u32[]{:S(2)}, u32[]{:S(2)}) collective-permute-start(bf16[128,1,224]{0,2,1:T(8,128)(2,1)S(1)} %get-tuple-element.84), channel_id=1, source_target_pairs={{32,0},{64,32},{96,64},{33,1},{65,33},{97,65},{34,2},{66,34},{98,6... | collective-permute-start | bytes 172040 | tf_op jit(solution)/shard_map/ppermute | solution.py:24
  46.7 37.6 %copy-start.74 = (s32[112]{0:T(128)}, s32[112]{0:T(128)S(1)}, u32[]{:S(2)}) copy-start(s32[112]{0:T(128)S(1)} %fusion.525) | copy-start | bytes 1348
  46.8 46.7 %copy-start.77 = (pred[112]{0:T(512)(128)(4,1)}, pred[112]{0:T(512)(128)(4,1)S(1)}, u32[]{:S(2)}) copy-start(pred[112]{0:T(512)(128)(4,1)S(1)} %compare_and_fusion.1) | copy-start | bytes 340
  47.3 66.4 %copy-start.60 = (f32[128]{0:T(128)}, f32[128]{0:T(128)S(1)}, u32[]{:S(2)}) copy-start(f32[128]{0:T(128)S(1)} %get-tuple-element.91) | copy-start | bytes 1540
  47.3 103.4 %copy-start.64 = (f32[128]{0:T(128)}, f32[128]{0:T(128)S(1)}, u32[]{:S(2)}) copy-start(f32[128]{0:T(128)S(1)} %get-tuple-element.90) | copy-start | bytes 1540
  47.3 152.7 %copy-start.70 = (f32[128]{0:T(128)}, f32[128]{0:T(128)S(1)}, u32[]{:S(2)}) copy-start(f32[128]{0:T(128)S(1)} %get-tuple-element.92) | copy-start | bytes 1540
  75.0 9.4 %copy-start.51 = (bf16[128,1,224]{0,2,1:T(8,128)(2,1)}, bf16[128,1,224]{0,2,1:T(8,128)(2,1)S(1)}, u32[]{:S(2)}) copy-start(bf16[128,1,224]{0,2,1:T(8,128)(2,1)S(1)} %collective-permute-done.8) | copy-start | bytes 172036
  114.6 19.0 %copy-start.9 = (bf16[128,14,448]{0,2,1:T(8,128)(2,1)}, bf16[128,14,448]{0,2,1:T(8,128)(2,1)S(1)}, u32[]{:S(2)}) copy-start(bf16[128,14,448]{0,2,1:T(8,128)(2,1)S(1)} %multiply_convert_fusion.1) | copy-start | bytes 4816900
  114.7 4.3 collective-permute-start
  116.1 5.5 collective-permute-start.1
  119.0 14.7 %copy-start.44 = (bf16[128,1,448]{0,2,1:T(8,128)(2,1)}, bf16[128,1,448]{0,2,1:T(8,128)(2,1)S(1)}, u32[]{:S(2)}) copy-start(bf16[128,1,448]{0,2,1:T(8,128)(2,1)S(1)} %collective-permute-done) | copy-start | bytes 344068
  121.6 9.0 %copy-start.42 = (bf16[128,1,448]{0,2,1:T(8,128)(2,1)}, bf16[128,1,448]{0,2,1:T(8,128)(2,1)S(1)}, u32[]{:S(2)}) copy-start(bf16[128,1,448]{0,2,1:T(8,128)(2,1)S(1)} %collective-permute-done.1) | copy-start | bytes 344068
  122.1 14.5 %copy-start.2 = (bf16[128,16,450]{0,2,1:T(8,128)(2,1)}, bf16[128,16,450]{0,2,1:T(8,128)(2,1)S(1)}, u32[]{:S(2)}) copy-start(bf16[128,16,450]{0,2,1:T(8,128)(2,1)S(1)} %fusion.12) | copy-start | bytes 5529604
  153.6 21.6 %copy-start.11 = (bf16[128,14,448]{0,2,1:T(8,128)(2,1)}, bf16[128,14,448]{0,2,1:T(8,128)(2,1)S(1)}, u32[]{:S(2)}) copy-start(bf16[128,14,448]{0,2,1:T(8,128)(2,1)S(1)} %multiply_convert_fusion) | copy-start | bytes 4816900
  153.6 5.4 collective-permute-start.2
  156.0 5.5 collective-permute-start.3
  162.0 16.2 %copy-start.5 = (bf16[128,16,450]{0,2,1:T(8,128)(2,1)}, bf16[128,16,450]{0,2,1:T(8,128)(2,1)S(1)}, u32[]{:S(2)}) copy-start(bf16[128,16,450]{0,2,1:T(8,128)(2,1)S(1)} %select_maximum_fusion.4) | copy-start | bytes 5529604
  201.4 16.8 %copy-start.27 = (bf16[128,7,224]{0,2,1:T(8,128)(2,1)}, bf16[128,7,224]{0,2,1:T(8,128)(2,1)S(1)}, u32[]{:S(2)}) copy-start(bf16[128,7,224]{0,2,1:T(8,128)(2,1)S(1)} %multiply_convert_fusion.3) | copy-start | bytes 1204228
  201.5 6.8 collective-permute-start.4
  204.9 4.9 collective-permute-start.5
  209.9 7.3 %copy-start.23 = (bf16[128,9,226]{0,2,1:T(8,128)(2,1)}, bf16[128,9,226]{0,2,1:T(8,128)(2,1)S(1)}, u32[]{:S(2)}) copy-start(bf16[128,9,226]{0,2,1:T(8,128)(2,1)S(1)} %fusion.284) | copy-start | bytes 1562116
  262.9 11.4 %copy-start.28 = (bf16[128,7,224]{0,2,1:T(8,128)(2,1)S(1)}, bf16[128,7,224]{0,2,1:T(8,128)(2,1)}, u32[]{:S(2)}) copy-start(bf16[128,7,224]{0,2,1:T(8,128)(2,1)} %copy-done.27) | copy-start | bytes 1204228
  264.8 12.2 %copy-start.25 = (bf16[128,7,224]{0,2,1:T(8,128)(2,1)}, bf16[128,7,224]{0,2,1:T(8,128)(2,1)S(1)}, u32[]{:S(2)}) copy-start(bf16[128,7,224]{0,2,1:T(8,128)(2,1)S(1)} %get-tuple-element.80) | copy-start | bytes 1204228
  265.1 11.8 %collective-permute-start.6 = (bf16[128,1,224]{0,2,1:T(8,128)(2,1)S(1)}, bf16[128,1,224]{0,2,1:T(8,128)(2,1)S(1)}, u32[]{:S(2)}, u32[]{:S(2)}) collective-permute-start(bf16[128,1,224]{0,2,1:T(8,128)(2,1)S(1)} %get-tuple-element.85), channel_id=1, source_target_pairs={{0,32},{32,64},{64,96},{1,33},{33,65},{65,97},{2,34},{34,66},{66,9... | collective-permute-start | bytes 172040 | tf_op jit(solution)/shard_map/ppermute | solution.py:22
  267.7 9.3 %collective-permute-start.7 = (bf16[128,1,224]{0,2,1:T(8,128)(2,1)S(1)}, bf16[128,1,224]{0,2,1:T(8,128)(2,1)S(1)}, u32[]{:S(2)}, u32[]{:S(2)}) collective-permute-start(bf16[128,1,224]{0,2,1:T(8,128)(2,1)S(1)} %get-tuple-element.86), channel_id=1, source_target_pairs={{32,0},{64,32},{96,64},{33,1},{65,33},{97,65},{34,2},{66,34},{98,6... | collective-permute-start | bytes 172040 | tf_op jit(solution)/shard_map/ppermute | solution.py:24
  269.0 11.1 %collective-permute-start.10 = (bf16[128,1,224]{0,2,1:T(8,128)(2,1)S(1)}, bf16[128,1,224]{0,2,1:T(8,128)(2,1)S(1)}, u32[]{:S(2)}, u32[]{:S(2)}) collective-permute-start(bf16[128,1,224]{0,2,1:T(8,128)(2,1)S(1)} %get-tuple-element.81), channel_id=1, source_target_pairs={{0,32},{32,64},{64,96},{1,33},{33,65},{65,97},{2,34},{34,66},{66,9... | collective-permute-start | bytes 172040 | tf_op jit(solution)/shard_map/ppermute | solution.py:22
  273.0 7.1 collective-permute-start.11
  303.4 38.7 %copy-start.16 = (f32[128,14,224,2]{0,3,2,1:T(2,128)}, f32[128,14,224,2]{0,3,2,1:T(2,128)S(1)}, u32[]{:S(2)}) copy-start(f32[128,14,224,2]{0,3,2,1:T(2,128)S(1)} %broadcast_in_dim.116) | copy-start | bytes 9633796
  318.2 8.3 %copy-start.12 = (bf16[128,14,448]{0,2,1:T(8,128)(2,1)S(1)}, bf16[128,14,448]{0,2,1:T(8,128)(2,1)}, u32[]{:S(2)}) copy-start(bf16[128,14,448]{0,2,1:T(8,128)(2,1)} %copy-done.11) | copy-start | bytes 4816900
  320.5 24.9 %collective-permute-start.13 = (bf16[128,1,448]{0,2,1:T(8,128)(2,1)}, bf16[128,1,448]{0,2,1:T(8,128)(2,1)S(1)}, u32[]{:S(2)}, u32[]{:S(2)}) collective-permute-start(bf16[128,1,448]{0,2,1:T(8,128)(2,1)} %get-tuple-element.73), channel_id=1, source_target_pairs={{32,0},{64,32},{96,64},{33,1},{65,33},{97,65},{34,2},{66,34},{98,6... | collective-permute-start | bytes 344072 | tf_op jit(solution)/shard_map/ppermute | solution.py:24
  321.8 23.6 %collective-permute-start.12 = (bf16[128,1,448]{0,2,1:T(8,128)(2,1)}, bf16[128,1,448]{0,2,1:T(8,128)(2,1)}, u32[]{:S(2)}, u32[]{:S(2)}) collective-permute-start(bf16[128,1,448]{0,2,1:T(8,128)(2,1)} %get-tuple-element.74), channel_id=1, source_target_pairs={{0,32},{32,64},{64,96},{1,33},{33,65},{65,97},{2,34},{34,66},{66,9... | collective-permute-start | bytes 344072 | tf_op jit(solution)/shard_map/ppermute | solution.py:22
  387.4 22.2 %copy-start.7 = (bf16[128,14,448]{0,2,1:T(8,128)(2,1)}, bf16[128,14,448]{0,2,1:T(8,128)(2,1)S(1)}, u32[]{:S(2)}) copy-start(bf16[128,14,448]{0,2,1:T(8,128)(2,1)S(1)} %fusion.6) | copy-start | bytes 4816900
  387.5 6.8 copy-start.3
  389.0 6.6 collective-permute-start.15
  390.3 5.8 collective-permute-start.14
  429.6 6.2 copy-start.50
  471.0 29.5 %copy-start.8 = (bf16[128,14,448]{0,2,1:T(8,128)(2,1)S(1)}, bf16[128,14,448]{0,2,1:T(8,128)(2,1)}, u32[]{:S(2)}) copy-start(bf16[128,14,448]{0,2,1:T(8,128)(2,1)} %copy-done.7) | copy-start | bytes 4816900
  471.0 220.8 %all-to-all-start.1 = ((bf16[128,2,64,128]{3,2,1,0:T(8,128)(2,1)}), bf16[128,2,64,128]{3,2,1,0:T(8,128)(2,1)}, u32[]{:S(2)}, u32[]{:S(2)}) async-start(bf16[128,2,64,128]{3,2,1,0:T(8,128)(2,1)} %bitcast.660), calls=%async_computation.1 | async-start | bytes 8388608 | tf_op jit(solution)/shard_map/all_to_all | solution.py:229
  500.5 187.9 %all-reduce.19.cloned.1.call-start = ((), (), s32[]{:S(2)}) async-start(), calls=%async_computation.2 | async-start | bytes 4718592 | tf_op jit(solution)/shard_map/psum | solution.py:249
  704.0 6.4 copy-start.72
  704.1 6.4 copy-start.73
  (52 other events, 133.9 us)
Sparse Core Ops, SparseCore 0:
  515.5 172.7 all-reduce.18
where the time goes:
time: 735 us; the launch traced here: 724 us
  matrix products  200 us (27%)
  blocking collectives  145 us (20%)
  waiting for transfers between devices  122 us (17%)
  local copies, waits for them, and re-layouts  89.1 us (12%)
  starting transfers between devices  78.3 us (11%)
  other arithmetic  72.3 us (10%)
  between operations  16 us (2%)
    psum x1, blocking collectives, body(): lax.psum((conv_terms, gain_terms, lift_term, interp_term), ('lat', 'patch'))  86.9 us
    dot_general x36, matrix products, conv_transpose(): jnp.einsum('oc,orw->crw', weights[offset], window, preferred_element_type...  81.6 us
    psum x1, waiting for transfers between devices, body(): lax.psum((conv_terms, gain_terms, lift_term, interp_term), ('lat', 'patch'))  80.2 us
    dot_general x36, matrix products, conv_apply(): jnp.einsum('oc,crw->orw', weights[offset], window, preferred_element_type...  69.1 us
    psum x8, blocking collectives, global_pair(): return lax.psum((first_sum, second_sum), 'lat')  58.6 us
    dot_general x36, matrix products, kernel_grad(): jnp.einsum('orw,crw->oc', gradient, window, preferred_element_type=jnp.fl...  35.5 us
    all_to_all x1, starting transfers between devices, body(): lax.all_to_all(placed.reshape(devices, capacity, coarse_chans, block_cell...  29.4 us
    ppermute x8, waiting for transfers between devices, padded_2(): lax.ppermute(tail, axis, [(i, (i + 1) % count) for i in range(ends)])  28.2 us
  transfers between devices with their start and end apart: 19, of which 7 were waited for; matrix products, arithmetic and copies ran while one was open for 10% of the time, Pallas kernels for 0%

commit v1 on v0

v1 whole, which is shorter than its diff:
```python
import math

import jax
import jax.numpy as jnp
from jax import lax
from jax.experimental import pallas as pl
from jax.experimental.pallas import tpu as pltpu
from jax.sharding import PartitionSpec as P

GROUPS = 32
EPSILON = 1e-05
BF = jnp.bfloat16
F32 = jnp.float32
BOTH = ("lat", "patch")
VMEM_BYTES = 56 * 1024 * 1024
STAT_ROWS = 16
SPAN = 4


def call(kernel, outs, scratch, scalars, args, name):
    smem = pl.BlockSpec(memory_space=pltpu.SMEM)
    vmem = pl.BlockSpec(memory_space=pltpu.VMEM)
    return pl.pallas_call(
        kernel,
        out_shape=[jax.ShapeDtypeStruct(s, d) for s, d in outs],
        in_specs=[smem] * len(scalars) + [vmem] * len(args),
        out_specs=[vmem] * len(outs),
        scratch_shapes=[pltpu.VMEM(s, d) for s, d in scratch],
        compiler_params=pltpu.CompilerParams(vmem_limit_bytes=VMEM_BYTES),
        name=name,
    )(*scalars, *args)


def fold8(x):
    return jnp.sum(x.reshape(x.shape[0] // 8, 8, x.shape[1]), axis=0)


def group_sum(v):
    lane = lax.broadcasted_iota(jnp.int32, v.shape, 1)
    n = v.shape[1]
    v = v + jnp.where(lane % 2 == 0, pltpu.roll(v, n - 1, 1), pltpu.roll(v, 1, 1))
    return v + jnp.where(lane % 4 < 2, pltpu.roll(v, n - 2, 1), pltpu.roll(v, 2, 1))


def split3(v):
    hi = v.astype(BF).astype(F32)
    mid = (v - hi).astype(BF).astype(F32)
    return hi, mid, v - hi - mid


def stat_block(first, second):
    row = lax.broadcasted_iota(jnp.int32, (STAT_ROWS, first.shape[1]), 0)
    block = jnp.zeros(row.shape, F32)
    for i, part in enumerate(split3(first) + split3(second)):
        block = jnp.where(row == i, part, block)
    return block.astype(BF)


def stat_pair(block):
    f = block.astype(F32)
    return f[0:1] + f[1:2] + f[2:3], f[3:4] + f[4:5] + f[5:6]


def total_pair(blocks):
    pairs = [stat_pair(b) for b in blocks]
    return sum(p[0] for p in pairs), sum(p[1] for p in pairs)


def put_row(dst, index, value):
    width, chans = value.shape
    cell = lax.broadcasted_iota(jnp.int32, value.shape, 0)
    left = jnp.where(cell == 0, 0.0, pltpu.roll(value, 1, 0))
    right = jnp.where(cell == width - 1, 0.0, pltpu.roll(value, width - 1, 0))
    dst[index, :, 0:chans] = left.astype(BF)
    dst[index, :, chans : 2 * chans] = value.astype(BF)
    dst[index, :, 2 * chans : 3 * chans] = right.astype(BF)


def conv_pairs(rows3, weights, height, emit, carry):
    chans = weights.shape[1] // 2
    table = weights[...]

    def step(j, carry):
        lhs = jnp.concatenate([rows3[2 * j + s] for s in range(SPAN)], axis=1)
        out = jnp.dot(lhs, table, preferred_element_type=F32)
        carry = emit(2 * j, out[:, :chans], carry)
        return emit(2 * j + 1, out[:, chans:], carry)

    carry = lax.fori_loop(0, height // 2, step, carry)
    if height % 2:
        lhs = jnp.concatenate([rows3[height - 1 + s] for s in range(3)], axis=1)
        out = jnp.dot(lhs, weights[0 : lhs.shape[1], 0:chans], preferred_element_type=F32)
        carry = emit(height - 1, out, carry)
    return carry


def sigm(y):
    return 0.5 * jnp.tanh(0.5 * y) + 0.5


def act_of(x, vec):
    y = x * vec[2:3] + vec[3:4]
    return y * sigm(y)


def act_grad(grad, x, vec):
    y = x * vec[2:3] + vec[3:4]
    sg = sigm(y)
    return grad * sg * (1.0 + y * (1.0 - sg)), (x - vec[0:1]) * vec[1:2]


def norm_vectors(up, down, opposite, own, gain, width, height, count):
    up_stats, down_stats = up[width : width + STAT_ROWS], down[width : width + STAT_ROWS]
    first, second = total_pair([own[...], up_stats, down_stats, opposite[...]])
    first = group_sum(jnp.broadcast_to(first, (8, first.shape[1])))
    second = group_sum(jnp.broadcast_to(second, first.shape))
    mean = first / count
    inv = lax.rsqrt(second / count - mean * mean + EPSILON)
    gain8 = jnp.broadcast_to(gain[...], mean.shape)
    scale = inv * gain8
    row = lax.broadcasted_iota(jnp.int32, mean.shape, 0)
    local = 1.0 / (width * height)
    up_mean = stat_pair(up_stats)[0] * local
    down_mean = stat_pair(down_stats)[0] * local
    vec = jnp.where(row == 0, mean, inv)
    for i, part in enumerate([scale, -mean * scale, gain8, up_mean, down_mean]):
        vec = jnp.where(row == i + 2, part, vec)
    return vec


def back_vectors(up, down, opposite, own, vec, width, count):
    stats = [own[...], opposite[...]]
    stats += [up[width : width + STAT_ROWS], down[width : width + STAT_ROWS]]
    first, second = total_pair(stats)
    first = group_sum(jnp.broadcast_to(first * vec[4:5], (8, first.shape[1])))
    second = group_sum(jnp.broadcast_to(second * vec[4:5], first.shape))
    return first[0:1] / count, second[0:1] / count


def norm_grad(grad, x, vec, first, second):
    gs, normed = act_grad(grad, x, vec)
    return vec[1:2] * (gs * vec[4:5] - first - normed * second)


def send_raw(to_up, to_down, block, top, bottom, sums, width, height):
    first = jnp.sum(sums[0], axis=0, keepdims=True)
    second = jnp.sum(sums[1], axis=0, keepdims=True)
    stats = stat_block(first, second)
    mean = stat_pair(stats)[0] * (1.0 / (width * height))
    to_up[0:width] = (top - mean).astype(BF)
    to_down[0:width] = (bottom - mean).astype(BF)
    to_up[width : width + STAT_ROWS] = stats
    to_down[width : width + STAT_ROWS] = stats
    block[...] = stats


def send_grad(to_up, to_down, block, top, bottom, sums, width):
    stats = stat_block(
        jnp.sum(sums[0], axis=0, keepdims=True), jnp.sum(sums[1], axis=0, keepdims=True)
    )
    to_up[0:width] = top.astype(BF)
    to_down[0:width] = bottom.astype(BF)
    to_up[width : width + STAT_ROWS] = stats
    to_down[width : width + STAT_ROWS] = stats
    block[...] = stats


def halo_raw(up, down, vec, width):
    above = up[0:width].astype(F32) + vec[5:6]
    below = down[0:width].astype(F32) + vec[6:7]
    return above, below


def zeros2(chans):
    return jnp.zeros((8, chans), F32), jnp.zeros((8, chans), F32)


def add_sums(sums, x):
    return sums[0] + fold8(x), sums[1] + fold8(x * x)


def route_kernel(me_ref, owners_ref, blocks_ref, out_ref):
    me = me_ref[0]
    slots, tiles = owners_ref.shape
    owners = owners_ref[...]
    mine = owners == me
    k = lax.broadcasted_iota(jnp.int32, (slots, slots), 0)
    j = lax.broadcasted_iota(jnp.int32, (slots, slots), 1)
    earlier = jnp.where(j < k, 1.0, 0.0).astype(BF)
    flags = jnp.where(mine, 1.0, 0.0)
    before = jnp.dot(earlier, flags.astype(BF), preferred_element_type=F32)
    blocks = blocks_ref[...].astype(F32)
    first = jnp.sum(jnp.where(mine & (before < 0.5), blocks, 0.0), axis=0, keepdims=True)
    second = jnp.sum(jnp.where(mine & (before > 0.5), blocks, 0.0), axis=0, keepdims=True)
    count = jnp.sum(flags, axis=0, keepdims=True)
    lane = lax.broadcasted_iota(jnp.int32, (slots, tiles), 1)
    slot = lax.broadcasted_iota(jnp.int32, (slots, tiles), 0)
    column = jnp.sum(jnp.where(lane == me, owners, 0).astype(F32), axis=1, keepdims=True)
    as_row = jnp.sum(jnp.where(lane == slot, column, 0.0), axis=0, keepdims=True)
    same = (column == as_row) & (slot < lane) & (lane < slots)
    position = jnp.sum(jnp.where(same, 1.0, 0.0), axis=0, keepdims=True)
    row = lax.broadcasted_iota(jnp.int32, (8, tiles), 0)
    out = jnp.where(row == 0, first, 0.0)
    for i, part in enumerate([second, count, as_row, position]):
        out = jnp.where(row == i + 1, part, out)
    out_ref[...] = out.astype(jnp.int32)


def send_kernel(route_ref, coarse_ref, interp_ref, out_ref):
    table = interp_ref[...]

    def step(d, _):
        pair = jnp.concatenate([coarse_ref[route_ref[0, d]], coarse_ref[route_ref[1, d]]], axis=0)
        piece = lax.dot_general(table, pair, (((1,), (1,)), ((), ())), preferred_element_type=F32)
        out_ref[d] = piece.astype(BF)
        return 0

    lax.fori_loop(0, out_ref.shape[0], step, 0, unroll=8)


def pool_kernel(grad_ref, pooled_ref, up_ref, down_ref, rows_ref):
    height, width, chans = grad_ref.shape
    half = width // 2

    def step(r, _):
        rows_ref[...] = grad_ref[2 * r] + grad_ref[2 * r + 1]
        pooled_ref[r] = rows_ref[pl.ds(0, half, stride=2)] + rows_ref[pl.ds(1, half, stride=2)]
        return 0

    lax.fori_loop(0, height // 2, step, 0)
    up_ref[0:width] = grad_ref[0].astype(BF)
    up_ref[width : width + half] = pooled_ref[0].astype(BF)
    down_ref[0:width] = grad_ref[height - 1].astype(BF)
    down_ref[width : width + half] = pooled_ref[height // 2 - 1].astype(BF)


def head_back_kernel(pooled_ref, up_ref, down_ref, edge_ref, weights_ref, grad_ref, rows3):
    height, width, chans = pooled_ref.shape
    start = up_ref.shape[0] - width
    put_row(rows3, 0, up_ref[start:].astype(F32) * edge_ref[0:1])
    put_row(rows3, height + 1, down_ref[start:].astype(F32) * edge_ref[1:2])

    def fill(r, _):
        put_row(rows3, r + 1, pooled_ref[r])
        return 0

    lax.fori_loop(0, height, fill, 0)

    def emit(r, value, carry):
        grad_ref[r] = value
        return carry

    conv_pairs(rows3, weights_ref, height, emit, 0)


def hidden_kernel(route_ref, arrived_ref, noisy_ref, lift_ref, hid_ref, cond_ref, up_ref, down_ref,
                  block_ref, line_ref):
    height, width, chans = noisy_ref.shape
    region = arrived_ref.shape[1]
    per_row = width // region
    upper = lax.broadcasted_iota(jnp.int32, (region, chans), 1) >= chans // 2
    table = lift_ref[...]

    def step(r, sums):
        for i in range(per_row):
            k = r * per_row + i
            piece = arrived_ref[route_ref[3, k]].astype(F32)
            keep = upper == (route_ref[4, k] > 0)
            line_ref[i * region : (i + 1) * region] = jnp.where(keep, piece, 0.0)
        cond = line_ref[...].astype(BF)
        cond_ref[r] = cond
        hidden = noisy_ref[r].astype(F32) + jnp.dot(cond, table, preferred_element_type=F32)
        hid_ref[r] = hidden
        return add_sums(sums, hidden)

    sums = lax.fori_loop(0, height, step, zeros2(chans))
    send_raw(up_ref, down_ref, block_ref, hid_ref[0], hid_ref[height - 1], sums, width, height)


def norm_rows(x_ref, vec, up_ref, down_ref, edge_ref, rows3, act_ref):
    height, width, chans = x_ref.shape
    above, below = halo_raw(up_ref, down_ref, vec, width)
    above = act_of(above, vec) * edge_ref[0:1]
    below = act_of(below, vec) * edge_ref[1:2]
    put_row(rows3, 0, above)
    put_row(rows3, height + 1, below)
    act_ref[0] = above.astype(BF)
    act_ref[height + 1] = below.astype(BF)

    def fill(r, _):
        value = act_of(x_ref[r], vec)
        put_row(rows3, r + 1, value)
        act_ref[r + 1] = value.astype(BF)
        return 0

    lax.fori_loop(0, height, fill, 0)


def make_first(count):
    def kernel(x_ref, up_ref, down_ref, opp_ref, own_ref, edge_ref, gain_ref, weights_ref,
               y_ref, act_ref, vec_ref, to_up, to_down, block_ref, rows3):
        height, width, chans = x_ref.shape
        vec = norm_vectors(up_ref, down_ref, opp_ref, own_ref, gain_ref, width, height, count)
        vec_ref[...] = vec
        norm_rows(x_ref, vec, up_ref, down_ref, edge_ref, rows3, act_ref)

        def emit(r, value, sums):
            y_ref[r] = value
            return add_sums(sums, value)

        sums = conv_pairs(rows3, weights_ref, height, emit, zeros2(chans))
        send_raw(to_up, to_down, block_ref, y_ref[0], y_ref[height - 1], sums, width, height)

    return kernel


def make_second(count):
    def kernel(y_ref, up_ref, down_ref, opp_ref, own_ref, edge_ref, gain_ref, weights_ref, hid_ref,
               level_ref, pooled_ref, act_ref, vec_ref, to_up, to_down, block_ref, rows3, line_ref):
        height, width, chans = y_ref.shape
        half = width // 2
        vec = norm_vectors(up_ref, down_ref, opp_ref, own_ref, gain_ref, width, height, count)
        vec_ref[...] = vec
        norm_rows(y_ref, vec, up_ref, down_ref, edge_ref, rows3, act_ref)
        table = weights_ref[...]

        def step(j, sums):
            lhs = jnp.concatenate([rows3[2 * j + s] for s in range(SPAN)], axis=1)
            out = jnp.dot(lhs, table, preferred_element_type=F32)
            one = hid_ref[2 * j] + out[:, :chans]
            two = hid_ref[2 * j + 1] + out[:, chans:]
            level_ref[2 * j] = one
            level_ref[2 * j + 1] = two
            line_ref[...] = one + two
            pooled = 0.25 * (line_ref[pl.ds(0, half, stride=2)] + line_ref[pl.ds(1, half, stride=2)])
            pooled_ref[j] = pooled
            return add_sums(sums, pooled)

        sums = lax.fori_loop(0, height // 2, step, zeros2(chans))
        last = height // 2 - 1
        send_raw(to_up, to_down, block_ref, pooled_ref[0], pooled_ref[last], sums, half, height // 2)

    return kernel


def make_turn(count):
    def kernel(y_ref, up_ref, down_ref, opp_ref, own_ref, edge_ref, gain_ref, grad_ref,
               act_ref, vec_ref, to_up, to_down, block_ref):
        height, width, chans = y_ref.shape
        vec = norm_vectors(up_ref, down_ref, opp_ref, own_ref, gain_ref, width, height, count)
        vec_ref[...] = vec
        above, below = halo_raw(up_ref, down_ref, vec, width)
        act_ref[0] = (act_of(above, vec) * edge_ref[0:1]).astype(BF)
        act_ref[height + 1] = (act_of(below, vec) * edge_ref[1:2]).astype(BF)

        def fill(r, sums):
            x = y_ref[r]
            y = x * vec[2:3] + vec[3:4]
            sg = sigm(y)
            act_ref[r + 1] = (y * sg).astype(BF)
            gs = grad_ref[r] * sg * (1.0 + y * (1.0 - sg))
            return sums[0] + fold8(gs), sums[1] + fold8(gs * (x - vec[0:1]) * vec[1:2])

        sums = lax.fori_loop(0, height, fill, zeros2(chans))
        send_grad(to_up, to_down, block_ref, grad_ref[0], grad_ref[height - 1], sums, width)

    return kernel


def tail_kernel(act_ref, weights_ref, pooled_ref, level_ref, out_ref, rows3, line_ref):
    height, width, chans = pooled_ref.shape

    def fill(r, _):
        put_row(rows3, r, act_ref[r].astype(F32))
        return 0

    lax.fori_loop(0, height + 2, fill, 0)

    def emit(r, value, carry):
        two = pooled_ref[r] + value
        line_ref[pl.ds(0, width, stride=2)] = two
        line_ref[pl.ds(1, width, stride=2)] = two
        wide = line_ref[...]
        out_ref[2 * r] = level_ref[2 * r] + wide
        out_ref[2 * r + 1] = level_ref[2 * r + 1] + wide
        return carry

    conv_pairs(rows3, weights_ref, height, emit, 0)


def back_conv(rows3, weights_ref, x_ref, vec, grad_ref, to_up, to_down, block_ref):
    height, width, chans = x_ref.shape

    def emit(r, value, sums):
        grad_ref[r] = value
        gs, normed = act_grad(value, x_ref[r], vec)
        return sums[0] + fold8(gs), sums[1] + fold8(gs * normed)

    sums = conv_pairs(rows3, weights_ref, height, emit, zeros2(chans))
    send_grad(to_up, to_down, block_ref, grad_ref[0], grad_ref[height - 1], sums, width)


def make_back_mid(count):
    def kernel(ga_ref, y_ref, yup_ref, ydown_ref, vec_ref, gup_ref, gdown_ref, opp_ref, own_ref,
               edge_ref, weights_ref, x_ref, xvec_ref,
               g_ref, out_ref, to_up, to_down, block_ref, rows3):
        height, width, chans = y_ref.shape
        vec = vec_ref[...]
        first, second = back_vectors(gup_ref, gdown_ref, opp_ref, own_ref, vec, width, count)
        above, below = halo_raw(yup_ref, ydown_ref, vec, width)
        g_above = norm_grad(gup_ref[0:width].astype(F32), above, vec, first, second)
        g_below = norm_grad(gdown_ref[0:width].astype(F32), below, vec, first, second)
        put_row(rows3, 0, g_above * edge_ref[0:1])
        put_row(rows3, height + 1, g_below * edge_ref[1:2])

        def fill(r, _):
            value = norm_grad(ga_ref[r], y_ref[r], vec, first, second)
            put_row(rows3, r + 1, value)
            g_ref[r] = value.astype(BF)
            return 0

        lax.fori_loop(0, height, fill, 0)
        back_conv(rows3, weights_ref, x_ref, xvec_ref[...], out_ref, to_up, to_down, block_ref)

    return kernel


def make_back_join(count):
    def kernel(ga_ref, p_ref, pup_ref, pdown_ref, pvec_ref, gup_ref, gdown_ref, opp_ref, own_ref,
               edge_ref, pg_ref, og_ref, oup_ref, odown_ref, weights_ref, x_ref, xvec_ref,
               level_ref, g_ref, out_ref, to_up, to_down, block_ref, rows3, line_ref):
        half_height, half, chans = p_ref.shape
        height, width, _ = og_ref.shape
        vec = pvec_ref[...]
        first, second = back_vectors(gup_ref, gdown_ref, opp_ref, own_ref, vec, half, count)

        def widened(value):
            line_ref[pl.ds(0, half, stride=2)] = value
            line_ref[pl.ds(1, half, stride=2)] = value
            return 0.25 * line_ref[...]

        above, below = halo_raw(pup_ref, pdown_ref, vec, half)
        g_above = norm_grad(gup_ref[0:half].astype(F32), above, vec, first, second)
        g_below = norm_grad(gdown_ref[0:half].astype(F32), below, vec, first, second)
        wide = widened(g_above + oup_ref[width : width + half].astype(F32))
        put_row(rows3, 0, (oup_ref[0:width].astype(F32) + wide) * edge_ref[0:1])
        wide = widened(g_below + odown_ref[width : width + half].astype(F32))
        put_row(rows3, height + 1, (odown_ref[0:width].astype(F32) + wide) * edge_ref[1:2])

        def fill(r, _):
            value = pg_ref[r] + norm_grad(ga_ref[r], p_ref[r], vec, first, second)
            wide = widened(value)
            for i in range(2):
                grad = og_ref[2 * r + i] + wide
                level_ref[2 * r + i] = grad
                put_row(rows3, 2 * r + i + 1, grad)
                g_ref[2 * r + i] = grad.astype(BF)
            return 0

        lax.fori_loop(0, half_height, fill, 0)
        back_conv(rows3, weights_ref, x_ref, xvec_ref[...], out_ref, to_up, to_down, block_ref)

    return kernel


def kernel_grad_kernel(g_ref, act_ref, out_ref, rows3, acc_ref):
    height, width, chans = g_ref.shape

    def fill(r, _):
        put_row(rows3, r, act_ref[r].astype(F32))
        return 0

    lax.fori_loop(0, height + 2, fill, 0)
    acc_ref[...] = jnp.zeros(acc_ref.shape, F32)

    def step(r, _):
        rhs = jnp.concatenate([rows3[r + s] for s in range(3)], axis=1)
        acc_ref[...] += lax.dot_general(
            g_ref[r], rhs, (((0,), (0,)), ((), ())), preferred_element_type=F32
        )
        return 0

    lax.fori_loop(0, height, step, 0)
    for tap in range(9):
        out_ref[tap] = acc_ref[:, tap * chans : (tap + 1) * chans].astype(out_ref.dtype)


def make_last(count):
    def kernel(route_ref, ga_ref, x_ref, vec_ref, gup_ref, gdown_ref, opp_ref, own_ref, level_ref,
               lift_ref, cond_ref, out_ref, lift_out, line_ref):
        height, width, chans = x_ref.shape
        region = out_ref.shape[1]
        per_row = width // region
        vec = vec_ref[...]
        first, second = back_vectors(gup_ref, gdown_ref, opp_ref, own_ref, vec, 0, count)
        upper = lax.broadcasted_iota(jnp.int32, (region, chans), 1) >= chans // 2
        table = lift_ref[...]
        lift_out[...] = jnp.zeros(lift_out.shape, F32)

        def clear(d, _):
            out_ref[d] = jnp.zeros((region, chans), BF)
            return 0

        lax.fori_loop(0, out_ref.shape[0], clear, 0, unroll=8)

        def step(r, _):
            grad = level_ref[r] + norm_grad(ga_ref[r], x_ref[r], vec, first, second)
            grad = grad.astype(BF)
            lift_out[...] += lax.dot_general(
                grad, cond_ref[r], (((0,), (0,)), ((), ())), preferred_element_type=F32
            )
            line_ref[...] = jnp.dot(grad, table, preferred_element_type=F32)
            for i in range(per_row):
                k = r * per_row + i
                d = route_ref[3, k]
                piece = line_ref[i * region : (i + 1) * region]
                keep = upper == (route_ref[4, k] > 0)
                out_ref[d] = jnp.where(keep, piece, out_ref[d].astype(F32)).astype(BF)
            return 0

        lax.fori_loop(0, height, step, 0)

    return kernel


def owner_kernel(route_ref, arrived_ref, coarse_ref, interp_ref, grad_ref, interp_out, sums_ref):
    tiles, region, lanes = arrived_ref.shape
    half = lanes // 2
    blocks = coarse_ref.shape[0]
    upper = lax.broadcasted_iota(jnp.int32, (region, lanes), 1) >= half

    def clear(b, _):
        sums_ref[b] = jnp.zeros((region, lanes), F32)
        return 0

    lax.fori_loop(0, blocks, clear, 0, unroll=8)

    def gather(d, _):
        piece = arrived_ref[d].astype(F32)
        count = route_ref[2, d]
        first, second = route_ref[0, d], route_ref[1, d]
        keep = jnp.logical_not(upper) & (count > 0)
        sums_ref[first] += jnp.where(keep, piece, 0.0)
        keep = upper & (count > 1)
        sums_ref[second] += jnp.where(keep, piece, 0.0)
        return 0

    lax.fori_loop(0, tiles, gather, 0, unroll=4)
    table = interp_ref[...]
    interp_out[...] = jnp.zeros(interp_out.shape, F32)

    def finish(b, _):
        total = sums_ref[b].astype(BF)
        wide = lax.dot_general(total, table, (((0,), (0,)), ((), ())), preferred_element_type=F32)
        grad_ref[b] = wide[:half] + wide[half:]
        pair = jnp.concatenate([coarse_ref[b], coarse_ref[b]], axis=0)
        interp_out[...] += jnp.dot(total, pair, preferred_element_type=F32)
        return 0

    lax.fori_loop(0, blocks, finish, 0, unroll=4)


def ring(x, shift):
    count = lax.axis_size("lat")
    return lax.ppermute(x, "lat", [(i, (i + shift) % count) for i in range(count)])


def exchange(to_up, to_down, block):
    return ring(to_down, 1), ring(to_up, -1), ring(block, 2), block


def pair_weights(taps):
    inner, outer = taps.shape[1], taps.shape[2]
    rows = taps.reshape(3, 3 * inner, outer)
    none = jnp.zeros((3 * inner, outer), taps.dtype)
    one = jnp.concatenate([rows[0], rows[1], rows[2], none], axis=0)
    two = jnp.concatenate([none, rows[0], rows[1], rows[2]], axis=0)
    return jnp.concatenate([one, two], axis=1)


def body(coarse, slot_owner, slot_block, interp, lift, conv_weights, gains, fine_noisy, out_grad):
    devices = lax.axis_size(BOTH)
    lat_count = lax.axis_size("lat")
    lat = lax.axis_index("lat")
    me = lax.axis_index(BOTH).astype(jnp.int32).reshape(1)
    noisy = jnp.transpose(fine_noisy[0], (1, 2, 0))
    grad = jnp.transpose(out_grad[0], (1, 2, 0))
    height, width, chans = noisy.shape
    half_height, half = height // 2, width // 2
    slots = slot_owner.shape[1]
    blocks, coarse_chans, cells = coarse.shape
    region = interp.shape[1]
    full_count = float(chans // GROUPS * height * width * lat_count)
    half_count = full_count / 4

    edge = jnp.stack([lat > 0, lat < lat_count - 1]).astype(F32)
    edge = jnp.broadcast_to(edge[:, None], (2, chans))
    forward = [pair_weights(jnp.transpose(conv_weights[i], (0, 2, 1))) for i in range(4)]
    backward = [pair_weights(conv_weights[i][::-1]) for i in range(4)]
    lift_rows = jnp.concatenate([lift.T, lift.T], axis=0)
    lift_cols = jnp.concatenate([lift, lift], axis=1)
    gain_rows = [gains[i : i + 1] for i in range(4)]

    full = (height, width, chans)
    small = (half_height, half, chans)
    full3 = ((height + 2, width, 3 * chans), BF)
    small3 = ((half_height + 2, half, 3 * chans), BF)
    line = ((width, chans), F32)
    vec_shape = ((8, chans), F32)
    full_act = ((height + 2, width, chans), BF)
    small_act = ((half_height + 2, half, chans), BF)
    full_msg = [((width + STAT_ROWS, chans), BF)] * 2 + [((STAT_ROWS, chans), BF)]
    small_msg = [((half + STAT_ROWS, chans), BF)] * 2 + [((STAT_ROWS, chans), BF)]

    edge_msg = ((width + half, chans), BF)
    pooled_grad, edge_up, edge_down = call(
        pool_kernel, [(small, F32), edge_msg, edge_msg], [line], [], [grad], "pool_grad"
    )
    grad_above, grad_below = ring(edge_down, 1), ring(edge_up, -1)

    (route,) = call(
        route_kernel,
        [((8, devices), jnp.int32)],
        [],
        [me],
        [slot_owner[:, :, 0].T, slot_block.T],
        "route",
    )
    (outgoing,) = call(
        send_kernel, [((devices, region, 2 * coarse_chans), BF)], [], [route], [coarse, interp.T], "send"
    )
    outgoing, grad_above, grad_below = lax.optimization_barrier((outgoing, grad_above, grad_below))
    arrived = lax.all_to_all(outgoing, BOTH, split_axis=0, concat_axis=0, tiled=True)
    (act_grad_d,) = call(
        head_back_kernel, [(small, F32)], [small3], [],
        [pooled_grad, grad_above, grad_below, edge, backward[3]], "back_d",
    )

    hidden, cond, *msg = call(
        hidden_kernel, [(full, F32), (full, BF)] + full_msg, [line], [route],
        [arrived, noisy, lift_rows], "hidden",
    )
    msg_h = exchange(*msg)
    conv_a, act_a, vec_a, *msg = call(
        make_first(full_count), [(full, F32), full_act, vec_shape] + full_msg, [full3], [],
        [hidden, *msg_h, edge, gain_rows[0], forward[0]], "conv_a",
    )
    msg_a = exchange(*msg)
    level, pooled, act_b, vec_b, *msg = call(
        make_second(full_count), [(full, F32), (small, F32), full_act, vec_shape] + small_msg,
        [full3, line], [], [conv_a, *msg_a, edge, gain_rows[1], forward[1], hidden], "conv_b",
    )
    msg_p = exchange(*msg)
    conv_c, act_c, vec_c, *msg = call(
        make_first(half_count), [(small, F32), small_act, vec_shape] + small_msg, [small3], [],
        [pooled, *msg_p, edge, gain_rows[2], forward[2]], "conv_c",
    )
    msg_c = exchange(*msg)
    act_d, vec_d, *msg = call(
        make_turn(half_count), [small_act, vec_shape] + small_msg, [], [],
        [conv_c, *msg_c, edge, gain_rows[3], act_grad_d], "turn_d",
    )
    back_d = exchange(*msg)
    (denoised,) = call(
        tail_kernel, [(full, F32)], [small3, line], [], [act_d, forward[3], pooled, level], "conv_d"
    )

    def taps_grad(g, act, name):
        rows3 = full3 if g.shape[1] == width else small3
        acc = ((chans, 9 * chans), F32)
        return call(kernel_grad_kernel, [((9, chans, chans), BF)], [rows3, acc], [], [g, act], name)[0]

    taps_d = taps_grad(pooled_grad.astype(BF), act_d, "taps_d")
    g_c, act_grad_c, *msg = call(
        make_back_mid(half_count), [(small, BF), (small, F32)] + small_msg, [small3], [],
        [act_grad_d, conv_c, msg_c[0], msg_c[1], vec_d, *back_d, edge, backward[2], pooled, vec_c],
        "back_c",
    )
    back_c = exchange(*msg)
    taps_c = taps_grad(g_c, act_c, "taps_c")
    grad_level, g_b, act_grad_b, *msg = call(
        make_back_join(half_count), [(full, F32), (full, BF), (full, F32)] + full_msg,
        [full3, line], [],
        [act_grad_c, pooled, msg_p[0], msg_p[1], vec_c, *back_c, edge, pooled_grad, grad,
         grad_above, grad_below, backward[1], conv_a, vec_b],
        "back_b",
    )
    back_b = exchange(*msg)
    taps_b = taps_grad(g_b, act_b, "taps_b")
    g_a, act_grad_a, *msg = call(
        make_back_mid(full_count), [(full, BF), (full, F32)] + full_msg, [full3], [],
        [act_grad_b, conv_a, msg_a[0], msg_a[1], vec_b, *back_b, edge, backward[0], hidden, vec_a],
        "back_a",
    )
    block = msg[2]
    back_a = (ring(block, 1), ring(block, -1), ring(block, 2), block)
    taps_a = taps_grad(g_a, act_a, "taps_a")
    placed, lift_term = call(
        make_last(full_count),
        [((devices, region, 2 * coarse_chans), BF), ((chans, 2 * coarse_chans), F32)], [line],
        [route],
        [act_grad_a, hidden, vec_a, *back_a, grad_level, lift_cols, cond], "grad_pieces",
    )

    gain_terms = jnp.concatenate(
        [sum(stat_pair(m[3])[1:]) for m in (back_a, back_b, back_c, back_d)], axis=0
    )
    lift_sum = lift_term[:, :coarse_chans] + lift_term[:, coarse_chans:]
    param_rows = chans * chans * 36 // (devices * chans)
    taps = jnp.concatenate(
        [t.reshape(-1, chans) for t in (taps_a, taps_b, taps_c, taps_d)]
    ).reshape(devices, param_rows, chans)
    extra = jnp.concatenate(
        [lift_sum.reshape(-1, chans), gain_terms,
         jnp.zeros((devices - lift_sum.size // chans - 4, chans), F32)]
    ).astype(BF).reshape(devices, 1, chans)
    params = jnp.concatenate([taps, extra], axis=1)
    returned = lax.all_to_all(placed, BOTH, split_axis=0, concat_axis=0, tiled=True)
    params = lax.all_to_all(params, BOTH, split_axis=0, concat_axis=0, tiled=True)
    coarse_grad, interp_term = call(
        owner_kernel, [((blocks, coarse_chans, cells), F32), ((region, cells), F32)],
        [((blocks, region, 2 * coarse_chans), F32)], [route], [returned, coarse, interp.T], "owner",
    )
    param_sum = jnp.sum(params.astype(F32), axis=0)
    interp_rows = jnp.concatenate([interp_term, jnp.zeros((devices - region, cells), F32)])
    interp_parts = lax.all_to_all(
        interp_rows.astype(BF).reshape(devices, 1, cells), BOTH, split_axis=0, concat_axis=0, tiled=True
    )
    interp_sum = jnp.sum(interp_parts.astype(F32), axis=0)
    scale = 1.0 / math.sqrt(height * width * devices)
    chunk = jnp.concatenate([param_sum, interp_sum], axis=0) * scale
    everything = lax.all_gather(chunk.astype(BF), BOTH).astype(F32)
    conv_total = everything[:, :param_rows].reshape(4, 9, chans, chans)
    extra_total = everything[:, param_rows]
    lift_count = lift_sum.size // chans
    lift_total = extra_total[:lift_count].reshape(lift_sum.shape)
    gain_total = extra_total[lift_count : lift_count + 4]
    interp_total = everything[:region, param_rows + 1].T
    return (
        jnp.transpose(denoised, (2, 0, 1))[None],
        coarse_grad,
        interp_total,
        lift_total,
        conv_total,
        gain_total,
    )


def solution(mesh):
    placed = (
        P(BOTH, None, None),
        P(),
        P(),
        P(),
        P(),
        P(),
        P(),
        P("patch", None, "lat", None),
        P("patch", None, "lat", None),
    )
    return jax.shard_map(
        body,
        mesh=mesh,
        in_specs=placed,
        out_specs=(
            P("patch", None, "lat", None),
            P(BOTH, None, None),
            P(),
            P(),
            P(),
            P(),
        ),
        check_vma=False,
    )
```

time: 735 us -> 395 us (0.54); the launches traced: 724 us -> 394 us
  matrix products: 200 us -> 0 us
  blocking collectives: 145 us -> 0 us
  Pallas kernels: 0 us -> 138 us
  local copies, waits for them, and re-layouts: 89.1 us -> 30.9 us
  other arithmetic: 72.3 us -> 22.1 us
  starting transfers between devices: 78.3 us -> 62.4 us
    dot_general x115 -> x0, matrix products: 200 us -> none  [the longest x36 81.6 us: conv_transpose(): jnp.einsum('oc,orw->crw', weights[offset], window, preferred_element_type...]
    psum x9 -> x0, blocking collectives: 145 us -> none  [the longest x1 86.9 us: body(): lax.psum((conv_terms, gain_terms, lift_term, interp_term), ('lat', 'patch'))]
    pallas_call x0 -> x19, Pallas kernels: none -> 138 us  [call(): pl.pallas_call(kernel, out_shape=[jax.ShapeDtypeStruct(s, d) for s, d in...]
    psum x1 -> x0, waiting for transfers between devices: 80.2 us -> none  [body(): lax.psum((conv_terms, gain_terms, lift_term, interp_term), ('lat', 'patch'))]
    all_to_all x2 -> x4, waiting for transfers between devices: 0.01 us -> 57.2 us  [the longest x1 22.5 us: body(): lax.all_to_all(placed, BOTH, split_axis=0, concat_axis=0, tiled=True)]
    all_gather x0 -> x1, waiting for transfers between devices: none -> 54.6 us  [body(): everything = lax.all_gather(chunk.astype(BF), BOTH).astype(F32)]
    ppermute x16 -> x26, waiting for transfers between devices: 41.9 us -> 13.4 us  [ring(): lax.ppermute(x, 'lat', [(i, (i + shift) % count) for i in range(count)])]
    convert_element_type x11 -> x8, other arithmetic: 23.9 us -> 1.71 us  [the longest x1 0.84 us: body(): taps_d = taps_grad(pooled_grad.astype(BF), act_d, 'taps_d')]
  transfers between devices with their start and end apart: 19 -> 31, of which waited for: 7 -> 10; matrix products, arithmetic and copies ran while one was open for 10% -> 9% of each run, Pallas kernels for 0% -> 12%
where the time goes in v1:
time: 395 us; the launch traced here: 394 us
  Pallas kernels  138 us (35%)
  waiting for transfers between devices  125 us (32%)
  starting transfers between devices  62.4 us (16%)
  local copies, waits for them, and re-layouts  30.9 us (8%)
  other arithmetic  22.1 us (6%)
  between operations  14.8 us (4%)
    pallas_call x19, Pallas kernels, call(): pl.pallas_call(kernel, out_shape=[jax.ShapeDtypeStruct(s, d) for s, d in...  138 us
    all_gather x1, waiting for transfers between devices, body(): everything = lax.all_gather(chunk.astype(BF), BOTH).astype(F32)  54.6 us
    ppermute x26, starting transfers between devices, ring(): lax.ppermute(x, 'lat', [(i, (i + shift) % count) for i in range(count)])  27.7 us
    all_to_all x1, waiting for transfers between devices, body(): lax.all_to_all(placed, BOTH, split_axis=0, concat_axis=0, tiled=True)  22.5 us
    all_to_all x1, starting transfers between devices, body(): lax.all_to_all(placed, BOTH, split_axis=0, concat_axis=0, tiled=True)  15.5 us
    concatenate x4, other arithmetic, pair_weights(): return jnp.concatenate([one, two], axis=1)  15.4 us
    all_to_all x1, waiting for transfers between devices, body(): lax.all_to_all(outgoing, BOTH, split_axis=0, concat_axis=0, tiled=True)  13.9 us
    ppermute x26, waiting for transfers between devices, ring(): lax.ppermute(x, 'lat', [(i, (i + shift) % count) for i in range(count)])  13.4 us
  transfers between devices with their start and end apart: 31, of which 10 were waited for; matrix products, arithmetic and copies ran while one was open for 9% of the time, Pallas kernels for 12%

profile of v1, /device:TPU:1, one launch (start us, length us, event | category | flops | bytes accessed | tf_op | source)
XLA Modules:
  0.0 393.7 jit_solution(871583103414188627)
XLA Ops:
  7.2 3.2 pool_grad.1
  10.3 2.1 collective-permute-start
  15.5 7.0 %send.1 = bf16[128,56,128]{2,1,0:T(8,128)(2,1)} custom-call(s32[8,128]{1,0:T(8,128)} %route.1.route_ref, bf16[64,64,128]{2,1,0:T(8,128)(2,1)} %coarse_ref.3, bf16[56,128]{1,0:T(8,128)(2,1)} %bitcast.144), custom_call_target="tpu_custom_call" | custom-call | tf_op jit(solution)/shard_map/send/pallas_call | solution.py:23
  23.2 10.0 %all-to-all-start = ((bf16[128,56,128]{2,1,0:T(8,128)(2,1)}), bf16[128,56,128]{2,1,0:T(8,128)(2,1)S(1)}, u32[]{:S(2)}, u32[]{:S(2)}) async-start(bf16[128,56,128]{2,1,0:T(8,128)(2,1)} %send.1), calls=%async_computation | async-start | bytes 3670016 | tf_op jit(solution)/shard_map/all_to_all | solution.py:633
  34.8 1.6 copy.56
  38.1 1.6 copy.57
  39.7 1.6 copy.54
  44.5 2.3 fusion.1
  46.8 13.9 %all-to-all-done.arrived_ref = bf16[128,56,128]{2,1,0:T(8,128)(2,1)S(1)} async-done(((bf16[128,56,128]{2,1,0:T(8,128)(2,1)}), bf16[128,56,128]{2,1,0:T(8,128)(2,1)S(1)}, u32[]{:S(2)}, u32[]{:S(2)}) %all-to-all-start) | async-done | bytes 1835040 | tf_op jit(solution)/shard_map/all_to_all | solution.py:633
  61.9 7.0 %hidden.1 = (f32[14,448,128]{2,1,0:T(8,128)}, bf16[14,448,128]{2,1,0:T(8,128)(2,1)}, bf16[464,128]{1,0:T(8,128)(2,1)}, bf16[464,128]{1,0:T(8,128)(2,1)}, bf16[16,128]{1,0:T(8,128)(2,1)}) custom-call(s32[8,128]{1,0:T(8,128)} %route.1.route_ref, bf16[128,56,128]{2,1,0:T(8,128)(2,1)} %copy-done.2, bf16[14,448,128]{2,1,0:T(8,128)(2,1)} %bitcast.113, ...), custom_call_target="tpu_custom_call" | custom-call | tf_op jit(solution)/shard_map/hidden/pallas_call | solution.py:23
  69.2 2.4 collective-permute-start.3
  72.2 4.1 %collective-permute-done.4.opp_ref = bf16[16,128]{1,0:T(8,128)(2,1)S(1)} collective-permute-done((bf16[16,128]{1,0:T(8,128)(2,1)}, bf16[16,128]{1,0:T(8,128)(2,1)S(1)}, u32[]{:S(2)}, u32[]{:S(2)}) %collective-permute-start.4) | collective-permute-done | bytes 4128 | tf_op jit(solution)/shard_map/ppermute | solution.py:565
  77.0 10.0 %conv_a.1 = (f32[14,448,128]{2,1,0:T(8,128)}, bf16[16,448,128]{2,1,0:T(8,128)(2,1)}, f32[8,128]{1,0:T(8,128)}, bf16[464,128]{1,0:T(8,128)(2,1)}, bf16[464,128]{1,0:T(8,128)(2,1)}, /*index=5*/bf16[16,128]{1,0:T(8,128)(2,1)}) custom-call(f32[14,448,128]{2,1,0:T(8,128)} %get-tuple-element.62.x_ref.hid_ref, bf16[464,128]{1,0:T(8,128)(2,1)} %copy-done.33, ...), custom_call_target="tpu_custom_call" | custom-call | tf_op jit(solution)/shard_map/conv_a/pallas_call | solution.py:23
  88.1 1.8 collective-permute-start.6
  93.1 12.1 %conv_b.1 = (f32[14,448,128]{2,1,0:T(8,128)}, f32[7,224,128]{2,1,0:T(8,128)}, bf16[16,448,128]{2,1,0:T(8,128)(2,1)}, f32[8,128]{1,0:T(8,128)}, bf16[240,128]{1,0...) custom-call(f32[14,448,128]{2,1,0:T(8,128)} %get-tuple-element.66.y_ref.x_ref, ...), custom_call_target="tpu_custom_call" | custom-call | tf_op jit(solution)/shard_map/conv_b/pallas_call | solution.py:23
  105.3 1.7 collective-permute-start.10
  109.6 4.3 %fusion.5 = (bf16[1536,256]{1,0:T(8,128)(2,1)}, bf16[1536,256]{1,0:T(8,128)(2,1)}) fusion(bf16[384,128]{1,0:T(8,128)(2,1)S(1)} %broadcast.21, bf16[384,128]{1,0:T(8,128)(2,1)S(1)} %bitcast.128, bf16[384,128]{1,0:T(8,128)(2,1)S(1)} %bitcast.130, bf16[384,128]{1,0:T(8,128)(2,1)S(1)} %bitcast.132, bf16[384,128]{1,0:T(8,128)(2,1)S(1)} %bitcast.124, ...), kind=kLoop, calls=%fused_computation.24 | loop fusion | flops 11796480 | bytes 2260992 | tf_op jit(solution)/shard_map/concatenate | solution.py:578
  114.8 4.5 %conv_c.1 = (f32[7,224,128]{2,1,0:T(8,128)}, bf16[9,224,128]{2,1,0:T(8,128)(2,1)}, f32[8,128]{1,0:T(8,128)}, bf16[240,128]{1,0:T(8,128)(2,1)}, bf16[240,128]{1,0:T(8,128)(2,1)}, /*index=5*/bf16[16,128]{1,0:T(8,128)(2,1)}) custom-call(f32[7,224,128]{2,1,0:T(8,128)} %get-tuple-element.70.x_ref.pooled_ref.p_ref, bf16[240,128]{1,0:T(8,128)(2,1)} %copy-done.31, ...), custom_call_target="tpu_custom_call" | custom-call | tf_op jit(solution)/shard_map/conv_c/pallas_call | solution.py:23
  121.0 1.8 collective-permute-start.12
  122.9 4.3 %fusion.7 = (bf16[1536,256]{1,0:T(8,128)(2,1)}, bf16[1536,256]{1,0:T(8,128)(2,1)}) fusion(bf16[384,128]{1,0:T(8,128)(2,1)S(1)} %broadcast.21, bf16[384,128]{1,0:T(8,128)(2,1)S(1)} %bitcast.134, bf16[384,128]{1,0:T(8,128)(2,1)S(1)} %bitcast.135, bf16[384,128]{1,0:T(8,128)(2,1)S(1)} %bitcast.127, bf16[384,128]{1,0:T(8,128)(2,1)S(1)} %bitcast.129, ...), kind=kLoop, calls=%fused_computation.26 | loop fusion | flops 11796480 | bytes 2260992 | tf_op jit(solution)/shard_map/concatenate | solution.py:578
  127.2 4.1 %back_d.1.grad_ref.ga_ref = f32[7,224,128]{2,1,0:T(8,128)} custom-call(f32[7,224,128]{2,1,0:T(8,128)} %get-tuple-element.78.pooled_ref.pg_ref, bf16[672,128]{1,0:T(8,128)(2,1)} %copy-done.10, bf16[672,128]{1,0:T(8,128)(2,1)} %copy-done.11, f32[2,128]{1,0:T(2,128)} %broadcast_in_dim.6.edge_ref, bf16[1536,256]{1,0:T(8,128)(2,1)} %get-tuple-element.153.weights_ref), custom_call_target="tpu_custom_call" | custom-call | tf_op jit(solution)/shard_map/back_d/pallas_call | solution.py:23
  132.0 3.1 turn_d.1
  135.1 2.7 collective-permute-start.15
  138.2 3.7 collective-permute-done.16.opp_ref
  142.6 5.4 %back_c.1 = (bf16[7,224,128]{2,1,0:T(8,128)(2,1)}, f32[7,224,128]{2,1,0:T(8,128)}, bf16[240,128]{1,0:T(8,128)(2,1)}, bf16[240,128]{1,0:T(8,128)(2,1)}, bf16[16,128]{1,0:T(8,128)(2,1)}) custom-call(f32[7,224,128]{2,1,0:T(8,128)} %back_d.1.grad_ref.ga_ref, f32[7,224,128]{2,1,0:T(8,128)} %get-tuple-element.74.y_ref, bf16[240,128]{1,0:T(8,128)(2,1)} %copy-done.29, ...), custom_call_target="tpu_custom_call" | custom-call | tf_op jit(solution)/shard_map/back_c/pallas_call | solution.py:23
  148.9 1.8 collective-permute-start.18
  150.8 4.4 %fusion.6 = (bf16[1536,256]{1,0:T(8,128)(2,1)}, bf16[1536,256]{1,0:T(8,128)(2,1)}) fusion(bf16[384,128]{1,0:T(8,128)(2,1)S(1)} %broadcast.21, bf16[384,128]{1,0:T(8,128)(2,1)S(1)} %bitcast.121, bf16[384,128]{1,0:T(8,128)(2,1)S(1)} %bitcast.122, bf16[384,128]{1,0:T(8,128)(2,1)S(1)} %bitcast.125, bf16[384,128]{1,0:T(8,128)(2,1)S(1)} %bitcast.119, ...), kind=kLoop, calls=%fused_computation.25 | loop fusion | flops 11796480 | bytes 2260992 | tf_op jit(solution)/shard_map/concatenate | solution.py:578
  155.8 13.8 %back_b.1 = (f32[14,448,128]{2,1,0:T(8,128)}, bf16[14,448,128]{2,1,0:T(8,128)(2,1)}, f32[14,448,128]{2,1,0:T(8,128)}, bf16[464,128]{1,0:T(8,128)(2,1)}, bf16[464...) custom-call(f32[7,224,128]{2,1,0:T(8,128)} %get-tuple-element.88.ga_ref, ...), custom_call_target="tpu_custom_call" | custom-call | tf_op jit(solution)/shard_map/back_b/pallas_call | solution.py:23
  169.6 2.7 collective-permute-start.21
  172.9 3.6 collective-permute-done.22.opp_ref
  177.1 13.8 %back_a.1 = (bf16[14,448,128]{2,1,0:T(8,128)(2,1)}, f32[14,448,128]{2,1,0:T(8,128)}, bf16[464,128]{1,0:T(8,128)(2,1)}, bf16[464,128]{1,0:T(8,128)(2,1)}, bf16[16,128]{1,0:T(8,128)(2,1)}) custom-call(f32[14,448,128]{2,1,0:T(8,128)} %get-tuple-element.93.ga_ref, f32[14,448,128]{2,1,0:T(8,128)} %get-tuple-element.66.y_ref.x_ref, bf16[464,128]{1,0:T(8,128)(2,1)} %copy-done.12, ...), custom_call_target="tpu_custom_call" | custom-call | tf_op jit(solution)/shard_map/back_a/pallas_call | solution.py:23
  194.5 4.2 %taps_d.1 = bf16[9,128,128]{2,1,0:T(8,128)(2,1)} custom-call(bf16[7,224,128]{2,1,0:T(8,128)(2,1)} %convert_element_type.51.g_ref, bf16[9,224,128]{2,1,0:T(8,128)(2,1)} %get-tuple-element.81.act_ref), custom_call_target="tpu_custom_call" | custom-call | tf_op jit(solution)/shard_map/taps_d/pallas_call | solution.py:23
  198.8 4.2 %taps_c.1 = bf16[9,128,128]{2,1,0:T(8,128)(2,1)} custom-call(bf16[7,224,128]{2,1,0:T(8,128)(2,1)} %get-tuple-element.108.g_ref, bf16[9,224,128]{2,1,0:T(8,128)(2,1)} %get-tuple-element.109.act_ref), custom_call_target="tpu_custom_call" | custom-call | tf_op jit(solution)/shard_map/taps_c/pallas_call | solution.py:23
  203.0 9.1 %taps_b.1 = bf16[9,128,128]{2,1,0:T(8,128)(2,1)} custom-call(bf16[14,448,128]{2,1,0:T(8,128)(2,1)} %get-tuple-element.106.g_ref, bf16[16,448,128]{2,1,0:T(8,128)(2,1)} %get-tuple-element.107.act_ref), custom_call_target="tpu_custom_call" | custom-call | tf_op jit(solution)/shard_map/taps_b/pallas_call | solution.py:23
  212.1 9.1 %taps_a.1 = bf16[9,128,128]{2,1,0:T(8,128)(2,1)} custom-call(bf16[14,448,128]{2,1,0:T(8,128)(2,1)} %get-tuple-element.104.g_ref, bf16[16,448,128]{2,1,0:T(8,128)(2,1)} %get-tuple-element.105.act_ref), custom_call_target="tpu_custom_call" | custom-call | tf_op jit(solution)/shard_map/taps_a/pallas_call | solution.py:23
  221.8 10.9 %grad_pieces.1 = (bf16[128,56,128]{2,1,0:T(8,128)(2,1)}, f32[128,128]{1,0:T(8,128)}) custom-call(s32[8,128]{1,0:T(8,128)} %route.1.route_ref, f32[14,448,128]{2,1,0:T(8,128)} %get-tuple-element.98.ga_ref, f32[14,448,128]{2,1,0:T(8,128)} %get-tuple-element.62.x_ref.hid_ref, f32[8,128]{1,0:T(8,128)} %get-tuple-element.97.xvec_ref.vec_ref, ...), custom_call_target="tpu_custom_call" | custom-call | tf_op jit(solution)/shard_map/grad_pieces/pallas_call | solution.py:23
  232.7 15.5 %all-to-all-start.1 = ((bf16[128,56,128]{2,1,0:T(8,128)(2,1)}), bf16[128,56,128]{2,1,0:T(8,128)(2,1)S(1)}, u32[]{:S(2)}, u32[]{:S(2)}) async-start(bf16[128,56,128]{2,1,0:T(8,128)(2,1)} %get-tuple-element.102), calls=%async_computation.1 | async-start | bytes 3670016 | tf_op jit(solution)/shard_map/all_to_all | solution.py:718
  249.3 2.2 reshape.249
  253.1 22.5 %all-to-all-done.1.arrived_ref = bf16[128,56,128]{2,1,0:T(8,128)(2,1)S(1)} async-done(((bf16[128,56,128]{2,1,0:T(8,128)(2,1)}), bf16[128,56,128]{2,1,0:T(8,128)(2,1)S(1)}, u32[]{:S(2)}, u32[]{:S(2)}) %all-to-all-start.1) | async-done | bytes 1835040 | tf_op jit(solution)/shard_map/all_to_all | solution.py:718
  275.6 4.7 %all-to-all-start.2 = ((bf16[128,37,128]{2,1,0:T(8,128)(2,1)}), bf16[128,37,128]{2,1,0:T(8,128)(2,1)S(1)}, u32[]{:S(2)}, u32[]{:S(2)}) async-start(bf16[128,37,128]{2,1,0:T(8,128)(2,1)} %pad_maximum_fusion.16), calls=%async_computation.2 | async-start | bytes 2621440 | tf_op jit(solution)/shard_map/all_to_all | solution.py:719
  280.3 8.9 %owner.1 = (f32[64,64,128]{2,1,0:T(8,128)}, f32[56,128]{1,0:T(8,128)}) custom-call(s32[8,128]{1,0:T(8,128)} %route.1.route_ref, bf16[128,56,128]{2,1,0:T(8,128)(2,1)} %copy-done.1, bf16[64,64,128]{2,1,0:T(8,128)(2,1)} %coarse_ref.3, bf16[56,128]{1,0:T(8,128)(2,1)} %bitcast.145), custom_call_target="tpu_custom_call" | custom-call | tf_op jit(solution)/shard_map/owner/pallas_call | solution.py:23
  290.7 11.7 %all-to-all-done.2 = bf16[128,37,128]{2,1,0:T(8,128)(2,1)S(1)} async-done(((bf16[128,37,128]{2,1,0:T(8,128)(2,1)}), bf16[128,37,128]{2,1,0:T(8,128)(2,1)S(1)}, u32[]{:S(2)}, u32[]{:S(2)}) %all-to-all-start.2) | async-done | bytes 1212448 | tf_op jit(solution)/shard_map/all_to_all | solution.py:719
  302.4 4.6 %all-to-all-start.3 = ((bf16[128,1,128]{2,1,0:T(2,128)(2,1)}), bf16[128,1,128]{2,1,0:T(2,128)(2,1)S(1)}, u32[]{:S(2)}, u32[]{:S(2)}) async-start(bf16[128,1,128]{2,1,0:T(2,128)(2,1)} %copy.68), calls=%async_computation.3 | async-start | bytes 131072 | tf_op jit(solution)/shard_map/all_to_all | solution.py:726
  307.3 9.2 %all-to-all-done.3 = bf16[128,1,128]{2,1,0:T(2,128)(2,1)S(1)} async-done(((bf16[128,1,128]{2,1,0:T(2,128)(2,1)}), bf16[128,1,128]{2,1,0:T(2,128)(2,1)S(1)}, u32[]{:S(2)}, u32[]{:S(2)}) %all-to-all-start.3) | async-done | bytes 32800 | tf_op jit(solution)/shard_map/all_to_all | solution.py:726
  317.2 6.2 %conv_d.1 = f32[14,448,128]{2,1,0:T(8,128)} custom-call(bf16[9,224,128]{2,1,0:T(8,128)(2,1)} %get-tuple-element.81.act_ref, bf16[1536,256]{1,0:T(8,128)(2,1)} %get-tuple-element.155.weights_ref, f32[7,224,128]{2,1,0:T(8,128)} %get-tuple-element.70.x_ref.pooled_ref.p_ref, f32[14,448,128]{2,1,0:T(8,128)} %get-tuple-element.82.level_ref), custom_call_target="tpu_custom_call" | custom-call | tf_op jit(solution)/shard_map/conv_d/pallas_call | solution.py:23
  323.4 54.6 %all-gather.2.cloned.1.call-done = bf16[128,38,128]{2,1,0:T(8,128)(2,1)} async-done(((bf16[1,38,128]{2,1,0:T(8,128)(2,1)}), bf16[128,38,128]{2,1,0:T(8,128)(2,1)}) %all-gather.2.cloned.1.call-update) | async-done | bytes 1245200 | tf_op jit(solution)/shard_map/all_gather | solution.py:732
  378.0 3.0 slice.394
  381.0 3.6 reshape.252
  (217 shorter events, 38.4 us)
Async XLA Ops:
  10.3 12.2 %collective-permute-start = (bf16[672,128]{1,0:T(8,128)(2,1)}, bf16[672,128]{1,0:T(8,128)(2,1)S(1)}, u32[]{:S(2)}, u32[]{:S(2)}) collective-permute-start(bf16[672,128]{1,0:T(8,128)(2,1)} %get-tuple-element.59), channel_id=1, source_target_pairs={{0,32},{32,64},{64,96},{96,0},{1,33},{33,65},{65,97},{97,1},{2,34}... | collective-permute-start | bytes 516104 | tf_op jit(solution)/shard_map/ppermute | solution.py:565
  12.5 10.1 %collective-permute-start.1 = (bf16[672,128]{1,0:T(8,128)(2,1)}, bf16[672,128]{1,0:T(8,128)(2,1)S(1)}, u32[]{:S(2)}, u32[]{:S(2)}) collective-permute-start(bf16[672,128]{1,0:T(8,128)(2,1)} %get-tuple-element.60), channel_id=1, source_target_pairs={{0,96},{32,0},{64,32},{96,64},{1,97},{33,1},{65,33},{97,65},{2,98}... | collective-permute-start | bytes 516104 | tf_op jit(solution)/shard_map/ppermute | solution.py:565
  22.5 10.7 %copy-start.4 = (bf16[4,9,128,128]{3,2,1,0:T(8,128)(2,1)S(1)}, bf16[4,9,128,128]{3,2,1,0:T(8,128)(2,1)}, u32[]{:S(2)}) copy-start(bf16[4,9,128,128]{3,2,1,0:T(8,128)(2,1)} %param.14) | copy-start | bytes 3538948
  23.2 37.4 %all-to-all-start = ((bf16[128,56,128]{2,1,0:T(8,128)(2,1)}), bf16[128,56,128]{2,1,0:T(8,128)(2,1)S(1)}, u32[]{:S(2)}, u32[]{:S(2)}) async-start(bf16[128,56,128]{2,1,0:T(8,128)(2,1)} %send.1), calls=%async_computation | async-start | bytes 3670016 | tf_op jit(solution)/shard_map/all_to_all | solution.py:633
  34.1 8.8 %copy-start.37 = (bf16[128,64]{0,1:T(8,128)(2,1)S(1)}, bf16[128,64]{0,1:T(8,128)(2,1)}, u32[]{:S(2)}) copy-start(bf16[128,64]{0,1:T(8,128)(2,1)} %param.13) | copy-start | bytes 49156
  61.9 9.7 %copy-start.56 = (f32[4,128]{1,0:T(4,128)S(1)}, f32[4,128]{1,0:T(4,128)}, u32[]{:S(2)}) copy-start(f32[4,128]{1,0:T(4,128)} %param.15) | copy-start | bytes 6148
  68.9 7.4 %collective-permute-start.2 = (bf16[464,128]{1,0:T(8,128)(2,1)}, bf16[464,128]{1,0:T(8,128)(2,1)S(1)}, u32[]{:S(2)}, u32[]{:S(2)}) collective-permute-start(bf16[464,128]{1,0:T(8,128)(2,1)} %get-tuple-element.63), channel_id=1, source_target_pairs={{0,32},{32,64},{64,96},{96,0},{1,33},{33,65},{65,97},{97,1},{2,34}... | collective-permute-start | bytes 356360 | tf_op jit(solution)/shard_map/ppermute | solution.py:565
  69.2 7.2 %collective-permute-start.3 = (bf16[464,128]{1,0:T(8,128)(2,1)}, bf16[464,128]{1,0:T(8,128)(2,1)S(1)}, u32[]{:S(2)}, u32[]{:S(2)}) collective-permute-start(bf16[464,128]{1,0:T(8,128)(2,1)} %get-tuple-element.64), channel_id=1, source_target_pairs={{0,96},{32,0},{64,32},{96,64},{1,97},{33,1},{65,33},{97,65},{2,98}... | collective-permute-start | bytes 356360 | tf_op jit(solution)/shard_map/ppermute | solution.py:565
  72.2 4.2 %collective-permute-start.4 = (bf16[16,128]{1,0:T(8,128)(2,1)}, bf16[16,128]{1,0:T(8,128)(2,1)S(1)}, u32[]{:S(2)}, u32[]{:S(2)}) collective-permute-start(bf16[16,128]{1,0:T(8,128)(2,1)} %get-tuple-element.65.own_ref), channel_id=1, source_target_pairs={{0,64},{32,96},{64,0},{96,32},{1,65},{33,97},{65,1},{97,33},{2,66}... | collective-permute-start | bytes 12296 | tf_op jit(solution)/shard_map/ppermute | solution.py:565
  77.0 12.9 %copy-start.7 = (bf16[9,128,128]{1,2,0:T(8,128)(2,1)S(1)}, bf16[9,128,128]{1,2,0:T(8,128)(2,1)}, u32[]{:S(2)}) copy-start(bf16[9,128,128]{1,2,0:T(8,128)(2,1)} %get-tuple-element.137) | copy-start | bytes 884740
  87.1 4.4 %collective-permute-start.7 = (bf16[16,128]{1,0:T(8,128)(2,1)}, bf16[16,128]{1,0:T(8,128)(2,1)S(1)}, u32[]{:S(2)}, u32[]{:S(2)}) collective-permute-start(bf16[16,128]{1,0:T(8,128)(2,1)} %get-tuple-element.69.own_ref), channel_id=1, source_target_pairs={{0,64},{32,96},{64,0},{96,32},{1,65},{33,97},{65,1},{97,33},{2,66}... | collective-permute-start | bytes 12296 | tf_op jit(solution)/shard_map/ppermute | solution.py:565
  87.2 5.2 %collective-permute-start.5 = (bf16[464,128]{1,0:T(8,128)(2,1)}, bf16[464,128]{1,0:T(8,128)(2,1)S(1)}, u32[]{:S(2)}, u32[]{:S(2)}) collective-permute-start(bf16[464,128]{1,0:T(8,128)(2,1)} %get-tuple-element.67), channel_id=1, source_target_pairs={{0,32},{32,64},{64,96},{96,0},{1,33},{33,65},{65,97},{97,1},{2,34}... | collective-permute-start | bytes 356360 | tf_op jit(solution)/shard_map/ppermute | solution.py:565
  88.1 4.3 %collective-permute-start.6 = (bf16[464,128]{1,0:T(8,128)(2,1)}, bf16[464,128]{1,0:T(8,128)(2,1)S(1)}, u32[]{:S(2)}, u32[]{:S(2)}) collective-permute-start(bf16[464,128]{1,0:T(8,128)(2,1)} %get-tuple-element.68), channel_id=1, source_target_pairs={{0,96},{32,0},{64,32},{96,64},{1,97},{33,1},{65,33},{97,65},{2,98}... | collective-permute-start | bytes 356360 | tf_op jit(solution)/shard_map/ppermute | solution.py:565
  105.2 8.8 %copy-start.20 = (bf16[3,128,128]{2,1,0:T(8,128)(2,1)S(1)}, bf16[3,128,128]{2,1,0:T(8,128)(2,1)}, u32[]{:S(2)}) copy-start(bf16[3,128,128]{2,1,0:T(8,128)(2,1)} %get-tuple-element.124) | copy-start | bytes 294916
  105.2 8.8 %copy-start.19 = (bf16[3,128,128]{2,1,0:T(8,128)(2,1)S(1)}, bf16[3,128,128]{2,1,0:T(8,128)(2,1)}, u32[]{:S(2)}) copy-start(bf16[3,128,128]{2,1,0:T(8,128)(2,1)} %get-tuple-element.131) | copy-start | bytes 294916
  105.2 8.8 %copy-start.18 = (bf16[3,128,128]{2,1,0:T(8,128)(2,1)S(1)}, bf16[3,128,128]{2,1,0:T(8,128)(2,1)}, u32[]{:S(2)}) copy-start(bf16[3,128,128]{2,1,0:T(8,128)(2,1)} %get-tuple-element.132) | copy-start | bytes 294916
  105.2 8.8 %copy-start.17 = (bf16[3,128,128]{2,1,0:T(8,128)(2,1)S(1)}, bf16[3,128,128]{2,1,0:T(8,128)(2,1)}, u32[]{:S(2)}) copy-start(bf16[3,128,128]{2,1,0:T(8,128)(2,1)} %get-tuple-element.133) | copy-start | bytes 294916
  105.2 8.8 %copy-start.16 = (bf16[3,128,128]{2,1,0:T(8,128)(2,1)S(1)}, bf16[3,128,128]{2,1,0:T(8,128)(2,1)}, u32[]{:S(2)}) copy-start(bf16[3,128,128]{2,1,0:T(8,128)(2,1)} %get-tuple-element.134) | copy-start | bytes 294916
  105.3 8.9 %collective-permute-start.10 = (bf16[16,128]{1,0:T(8,128)(2,1)}, bf16[16,128]{1,0:T(8,128)(2,1)S(1)}, u32[]{:S(2)}, u32[]{:S(2)}) collective-permute-start(bf16[16,128]{1,0:T(8,128)(2,1)} %get-tuple-element.73.own_ref), channel_id=1, source_target_pairs={{0,64},{32,96},{64,0},{96,32},{1,65},{33,97},{65,1},{97,33},{2,66}... | collective-permute-start | bytes 12296 | tf_op jit(solution)/shard_map/ppermute | solution.py:565
  107.0 7.2 %collective-permute-start.8 = (bf16[240,128]{1,0:T(8,128)(2,1)}, bf16[240,128]{1,0:T(8,128)(2,1)S(1)}, u32[]{:S(2)}, u32[]{:S(2)}) collective-permute-start(bf16[240,128]{1,0:T(8,128)(2,1)} %get-tuple-element.71), channel_id=1, source_target_pairs={{0,32},{32,64},{64,96},{96,0},{1,33},{33,65},{65,97},{97,1},{2,34}... | collective-permute-start | bytes 184328 | tf_op jit(solution)/shard_map/ppermute | solution.py:565
  108.6 5.6 %collective-permute-start.9 = (bf16[240,128]{1,0:T(8,128)(2,1)}, bf16[240,128]{1,0:T(8,128)(2,1)S(1)}, u32[]{:S(2)}, u32[]{:S(2)}) collective-permute-start(bf16[240,128]{1,0:T(8,128)(2,1)} %get-tuple-element.72), channel_id=1, source_target_pairs={{0,96},{32,0},{64,32},{96,64},{1,97},{33,1},{65,33},{97,65},{2,98}... | collective-permute-start | bytes 184328 | tf_op jit(solution)/shard_map/ppermute | solution.py:565
  119.3 12.0 %collective-permute-start.13 = (bf16[16,128]{1,0:T(8,128)(2,1)}, bf16[16,128]{1,0:T(8,128)(2,1)S(1)}, u32[]{:S(2)}, u32[]{:S(2)}) collective-permute-start(bf16[16,128]{1,0:T(8,128)(2,1)} %get-tuple-element.77.own_ref), channel_id=1, source_target_pairs={{0,64},{32,96},{64,0},{96,32},{1,65},{33,97},{65,1},{97,33},{2,66}... | collective-permute-start | bytes 12296 | tf_op jit(solution)/shard_map/ppermute | solution.py:565
  120.2 11.1 %collective-permute-start.11 = (bf16[240,128]{1,0:T(8,128)(2,1)}, bf16[240,128]{1,0:T(8,128)(2,1)S(1)}, u32[]{:S(2)}, u32[]{:S(2)}) collective-permute-start(bf16[240,128]{1,0:T(8,128)(2,1)} %get-tuple-element.75), channel_id=1, source_target_pairs={{0,32},{32,64},{64,96},{96,0},{1,33},{33,65},{65,97},{97,1},{2,34}... | collective-permute-start | bytes 184328 | tf_op jit(solution)/shard_map/ppermute | solution.py:565
  121.0 10.3 %collective-permute-start.12 = (bf16[240,128]{1,0:T(8,128)(2,1)}, bf16[240,128]{1,0:T(8,128)(2,1)S(1)}, u32[]{:S(2)}, u32[]{:S(2)}) collective-permute-start(bf16[240,128]{1,0:T(8,128)(2,1)} %get-tuple-element.76), channel_id=1, source_target_pairs={{0,96},{32,0},{64,32},{96,64},{1,97},{33,1},{65,33},{97,65},{2,98}... | collective-permute-start | bytes 184328 | tf_op jit(solution)/shard_map/ppermute | solution.py:565
  135.1 6.9 %collective-permute-start.14 = (bf16[240,128]{1,0:T(8,128)(2,1)}, bf16[240,128]{1,0:T(8,128)(2,1)S(1)}, u32[]{:S(2)}, u32[]{:S(2)}) collective-permute-start(bf16[240,128]{1,0:T(8,128)(2,1)} %get-tuple-element.84), channel_id=1, source_target_pairs={{0,32},{32,64},{64,96},{96,0},{1,33},{33,65},{65,97},{97,1},{2,34}... | collective-permute-start | bytes 184328 | tf_op jit(solution)/shard_map/ppermute | solution.py:565
  135.1 6.9 %collective-permute-start.15 = (bf16[240,128]{1,0:T(8,128)(2,1)}, bf16[240,128]{1,0:T(8,128)(2,1)S(1)}, u32[]{:S(2)}, u32[]{:S(2)}) collective-permute-start(bf16[240,128]{1,0:T(8,128)(2,1)} %get-tuple-element.85), channel_id=1, source_target_pairs={{0,96},{32,0},{64,32},{96,64},{1,97},{33,1},{65,33},{97,65},{2,98}... | collective-permute-start | bytes 184328 | tf_op jit(solution)/shard_map/ppermute | solution.py:565
  137.8 4.2 %collective-permute-start.16 = (bf16[16,128]{1,0:T(8,128)(2,1)}, bf16[16,128]{1,0:T(8,128)(2,1)S(1)}, u32[]{:S(2)}, u32[]{:S(2)}) collective-permute-start(bf16[16,128]{1,0:T(8,128)(2,1)} %get-tuple-element.86.own_ref), channel_id=1, source_target_pairs={{0,64},{32,96},{64,0},{96,32},{1,65},{33,97},{65,1},{97,33},{2,66}... | collective-permute-start | bytes 12296 | tf_op jit(solution)/shard_map/ppermute | solution.py:565
  148.0 7.1 %collective-permute-start.19 = (bf16[16,128]{1,0:T(8,128)(2,1)}, bf16[16,128]{1,0:T(8,128)(2,1)S(1)}, u32[]{:S(2)}, u32[]{:S(2)}) collective-permute-start(bf16[16,128]{1,0:T(8,128)(2,1)} %get-tuple-element.91.own_ref), channel_id=1, source_target_pairs={{0,64},{32,96},{64,0},{96,32},{1,65},{33,97},{65,1},{97,33},{2,66}... | collective-permute-start | bytes 12296 | tf_op jit(solution)/shard_map/ppermute | solution.py:565
  148.0 7.1 %collective-permute-start.17 = (bf16[240,128]{1,0:T(8,128)(2,1)}, bf16[240,128]{1,0:T(8,128)(2,1)S(1)}, u32[]{:S(2)}, u32[]{:S(2)}) collective-permute-start(bf16[240,128]{1,0:T(8,128)(2,1)} %get-tuple-element.89), channel_id=1, source_target_pairs={{0,32},{32,64},{64,96},{96,0},{1,33},{33,65},{65,97},{97,1},{2,34}... | collective-permute-start | bytes 184328 | tf_op jit(solution)/shard_map/ppermute | solution.py:565
  148.9 6.2 %collective-permute-start.18 = (bf16[240,128]{1,0:T(8,128)(2,1)}, bf16[240,128]{1,0:T(8,128)(2,1)S(1)}, u32[]{:S(2)}, u32[]{:S(2)}) collective-permute-start(bf16[240,128]{1,0:T(8,128)(2,1)} %get-tuple-element.90), channel_id=1, source_target_pairs={{0,96},{32,0},{64,32},{96,64},{1,97},{33,1},{65,33},{97,65},{2,98}... | collective-permute-start | bytes 184328 | tf_op jit(solution)/shard_map/ppermute | solution.py:565
  169.5 6.9 %collective-permute-start.20 = (bf16[464,128]{1,0:T(8,128)(2,1)}, bf16[464,128]{1,0:T(8,128)(2,1)S(1)}, u32[]{:S(2)}, u32[]{:S(2)}) collective-permute-start(bf16[464,128]{1,0:T(8,128)(2,1)} %get-tuple-element.94), channel_id=1, source_target_pairs={{0,32},{32,64},{64,96},{96,0},{1,33},{33,65},{65,97},{97,1},{2,34}... | collective-permute-start | bytes 356360 | tf_op jit(solution)/shard_map/ppermute | solution.py:565
  169.6 6.8 %collective-permute-start.21 = (bf16[464,128]{1,0:T(8,128)(2,1)}, bf16[464,128]{1,0:T(8,128)(2,1)S(1)}, u32[]{:S(2)}, u32[]{:S(2)}) collective-permute-start(bf16[464,128]{1,0:T(8,128)(2,1)} %get-tuple-element.95), channel_id=1, source_target_pairs={{0,96},{32,0},{64,32},{96,64},{1,97},{33,1},{65,33},{97,65},{2,98}... | collective-permute-start | bytes 356360 | tf_op jit(solution)/shard_map/ppermute | solution.py:565
  172.3 4.2 %collective-permute-start.22 = (bf16[16,128]{1,0:T(8,128)(2,1)}, bf16[16,128]{1,0:T(8,128)(2,1)S(1)}, u32[]{:S(2)}, u32[]{:S(2)}) collective-permute-start(bf16[16,128]{1,0:T(8,128)(2,1)} %get-tuple-element.96.own_ref), channel_id=1, source_target_pairs={{0,64},{32,96},{64,0},{96,32},{1,65},{33,97},{65,1},{97,33},{2,66}... | collective-permute-start | bytes 12296 | tf_op jit(solution)/shard_map/ppermute | solution.py:565
  177.1 16.6 %copy-start.3 = (f32[7,224,128]{2,1,0:T(8,128)S(1)}, f32[7,224,128]{2,1,0:T(8,128)}, u32[]{:S(2)}) copy-start(f32[7,224,128]{2,1,0:T(8,128)} %get-tuple-element.78.pooled_ref.pg_ref) | copy-start | bytes 2408452
  177.1 17.4 %copy-start.42 = (bf16[16,128]{1,0:T(8,128)(2,1)S(1)}, bf16[16,128]{1,0:T(8,128)(2,1)}, u32[]{:S(2)}) copy-start(bf16[16,128]{1,0:T(8,128)(2,1)} %get-tuple-element.86.own_ref) | copy-start | bytes 12292
  191.0 30.2 %collective-permute-start.25 = (bf16[16,128]{1,0:T(8,128)(2,1)}, bf16[16,128]{1,0:T(8,128)(2,1)S(1)}, u32[]{:S(2)}, u32[]{:S(2)}) collective-permute-start(bf16[16,128]{1,0:T(8,128)(2,1)} %get-tuple-element.99.own_ref), channel_id=1, source_target_pairs={{0,64},{32,96},{64,0},{96,32},{1,65},{33,97},{65,1},{97,33},{2,66}... | collective-permute-start | bytes 12296 | tf_op jit(solution)/shard_map/ppermute | solution.py:565
  191.5 29.6 %collective-permute-start.24 = (bf16[16,128]{1,0:T(8,128)(2,1)}, bf16[16,128]{1,0:T(8,128)(2,1)S(1)}, u32[]{:S(2)}, u32[]{:S(2)}) collective-permute-start(bf16[16,128]{1,0:T(8,128)(2,1)} %get-tuple-element.99.own_ref), channel_id=1, source_target_pairs={{0,96},{32,0},{64,32},{96,64},{1,97},{33,1},{65,33},{97,65},{2,98}... | collective-permute-start | bytes 12296 | tf_op jit(solution)/shard_map/ppermute | solution.py:565
  192.3 28.9 %collective-permute-start.23 = (bf16[16,128]{1,0:T(8,128)(2,1)}, bf16[16,128]{1,0:T(8,128)(2,1)S(1)}, u32[]{:S(2)}, u32[]{:S(2)}) collective-permute-start(bf16[16,128]{1,0:T(8,128)(2,1)} %get-tuple-element.99.own_ref), channel_id=1, source_target_pairs={{0,32},{32,64},{64,96},{96,0},{1,33},{33,65},{65,97},{97,1},{2,34}... | collective-permute-start | bytes 12296 | tf_op jit(solution)/shard_map/ppermute | solution.py:565
  193.7 9.3 %copy-start.44 = (bf16[16,128]{1,0:T(8,128)(2,1)S(1)}, bf16[16,128]{1,0:T(8,128)(2,1)}, u32[]{:S(2)}) copy-start(bf16[16,128]{1,0:T(8,128)(2,1)} %get-tuple-element.96.own_ref) | copy-start | bytes 12292
  203.0 9.1 %copy-start.45 = (bf16[16,128]{1,0:T(8,128)(2,1)S(1)}, bf16[16,128]{1,0:T(8,128)(2,1)}, u32[]{:S(2)}) copy-start(bf16[16,128]{1,0:T(8,128)(2,1)} %get-tuple-element.99.own_ref) | copy-start | bytes 12292
  232.6 15.5 %copy-start.5 = (bf16[9,128,128]{2,1,0:T(8,128)(2,1)S(1)}, bf16[9,128,128]{2,1,0:T(8,128)(2,1)}, u32[]{:S(2)}) copy-start(bf16[9,128,128]{2,1,0:T(8,128)(2,1)} %taps_b.1) | copy-start | bytes 884740
  232.6 15.5 %copy-start.6 = (bf16[9,128,128]{2,1,0:T(8,128)(2,1)S(1)}, bf16[9,128,128]{2,1,0:T(8,128)(2,1)}, u32[]{:S(2)}) copy-start(bf16[9,128,128]{2,1,0:T(8,128)(2,1)} %taps_a.1) | copy-start | bytes 884740
  232.6 15.5 %copy-start.8 = (bf16[9,128,128]{2,1,0:T(8,128)(2,1)S(1)}, bf16[9,128,128]{2,1,0:T(8,128)(2,1)}, u32[]{:S(2)}) copy-start(bf16[9,128,128]{2,1,0:T(8,128)(2,1)} %taps_d.1) | copy-start | bytes 884740
  232.7 15.5 %copy-start.9 = (bf16[9,128,128]{2,1,0:T(8,128)(2,1)S(1)}, bf16[9,128,128]{2,1,0:T(8,128)(2,1)}, u32[]{:S(2)}) copy-start(bf16[9,128,128]{2,1,0:T(8,128)(2,1)} %taps_c.1) | copy-start | bytes 884740
  232.7 43.0 %all-to-all-start.1 = ((bf16[128,56,128]{2,1,0:T(8,128)(2,1)}), bf16[128,56,128]{2,1,0:T(8,128)(2,1)S(1)}, u32[]{:S(2)}, u32[]{:S(2)}) async-start(bf16[128,56,128]{2,1,0:T(8,128)(2,1)} %get-tuple-element.102), calls=%async_computation.1 | async-start | bytes 3670016 | tf_op jit(solution)/shard_map/all_to_all | solution.py:718
  275.6 26.7 %all-to-all-start.2 = ((bf16[128,37,128]{2,1,0:T(8,128)(2,1)}), bf16[128,37,128]{2,1,0:T(8,128)(2,1)S(1)}, u32[]{:S(2)}, u32[]{:S(2)}) async-start(bf16[128,37,128]{2,1,0:T(8,128)(2,1)} %pad_maximum_fusion.16), calls=%async_computation.2 | async-start | bytes 2621440 | tf_op jit(solution)/shard_map/all_to_all | solution.py:719
  302.4 14.1 %all-to-all-start.3 = ((bf16[128,1,128]{2,1,0:T(2,128)(2,1)}), bf16[128,1,128]{2,1,0:T(2,128)(2,1)S(1)}, u32[]{:S(2)}, u32[]{:S(2)}) async-start(bf16[128,1,128]{2,1,0:T(2,128)(2,1)} %copy.68), calls=%async_computation.3 | async-start | bytes 131072 | tf_op jit(solution)/shard_map/all_to_all | solution.py:726
  307.0 71.0 %all-gather.2.cloned.1.call-start = ((), (), s32[]{:S(2)}) async-start(), calls=%async_computation.4 | async-start | bytes 1320960 | tf_op jit(solution)/shard_map/all_gather | solution.py:732
  (40 other events, 64.1 us)
Sparse Core Ops, SparseCore 0:
  317.4 60.6 all-gather.1

commit v2 on v1

--- a/solution.py
+++ b/solution.py
@@ -12,7 +12,7 @@
 BF = jnp.bfloat16
 F32 = jnp.float32
 BOTH = ("lat", "patch")
-VMEM_BYTES = 56 * 1024 * 1024
+VMEM_BYTES = 30 * 1024 * 1024
 STAT_ROWS = 16
 SPAN = 4
 
@@ -76,20 +76,46 @@
     dst[index, :, 2 * chans : 3 * chans] = right.astype(BF)
 
 
-def conv_pairs(rows3, weights, height, emit, carry):
-    chans = weights.shape[1] // 2
-    table = weights[...]
-
-    def step(j, carry):
+def build_table(table, weights, flipped):
+    chans = weights.shape[2]
+    span = 3 * chans
+    blank = jnp.zeros((span, chans), BF)
+    table[0:span, chans : 2 * chans] = blank
+    table[3 * span : 4 * span, 0:chans] = blank
+    for tap in range(9):
+        value = weights[8 - tap if flipped else tap]
+        table[tap * chans : (tap + 1) * chans, 0:chans] = value
+        table[span + tap * chans : span + (tap + 1) * chans, chans : 2 * chans] = value
+
+
+def conv_pairs(rows3, table, height, fill, emit, carry):
+    chans = table.shape[1] // 2
+
+    def pair(j):
         lhs = jnp.concatenate([rows3[2 * j + s] for s in range(SPAN)], axis=1)
-        out = jnp.dot(lhs, table, preferred_element_type=F32)
+        return jnp.dot(lhs, table[...], preferred_element_type=F32)
+
+    def both(j, out, carry):
         carry = emit(2 * j, out[:, :chans], carry)
         return emit(2 * j + 1, out[:, chans:], carry)
 
-    carry = lax.fori_loop(0, height // 2, step, carry)
+    mixed = (height - 3) // 2
+    for r in range(1, 4):
+        fill(r)
+    for r in range(4 + 2 * mixed, height + 1):
+        fill(r)
+
+    def step(j, carry):
+        out = pair(j)
+        fill(2 * j + 4)
+        fill(2 * j + 5)
+        return both(j, out, carry)
+
+    carry = lax.fori_loop(0, mixed, step, carry)
+    carry = lax.fori_loop(mixed, height // 2, lambda j, c: both(j, pair(j), c), carry)
     if height % 2:
         lhs = jnp.concatenate([rows3[height - 1 + s] for s in range(3)], axis=1)
-        out = jnp.dot(lhs, weights[0 : lhs.shape[1], 0:chans], preferred_element_type=F32)
+        out = jnp.dot(lhs, table[0 : lhs.shape[1], 0:chans], preferred_element_type=F32)
         carry = emit(height - 1, out, carry)
     return carry
 
@@ -206,13 +232,27 @@
     out_ref[...] = out.astype(jnp.int32)
 
 
-def send_kernel(route_ref, coarse_ref, interp_ref, out_ref):
+def send_kernel(route_ref, coarse_ref, interp_ref, out_ref, low_ref, high_ref):
     table = interp_ref[...]
+    region = table.shape[0]
+    blocks, chans, _ = coarse_ref.shape
+    upper = lax.broadcasted_iota(jnp.int32, (region, 2 * chans), 1) >= chans
+
+    def pieces(b, _):
+        pair = coarse_ref[pl.ds(2 * b, 2)].reshape(2 * chans, coarse_ref.shape[2])
+        piece = lax.dot_general(table, pair, (((1,), (1,)), ((), ())), preferred_element_type=F32)
+        turned = pltpu.roll(piece, chans, 1)
+        low_ref[2 * b] = piece
+        high_ref[2 * b] = turned
+        low_ref[2 * b + 1] = turned
+        high_ref[2 * b + 1] = piece
+        return 0
+
+    lax.fori_loop(0, blocks // 2, pieces, 0, unroll=4)
 
     def step(d, _):
-        pair = jnp.concatenate([coarse_ref[route_ref[0, d]], coarse_ref[route_ref[1, d]]], axis=0)
-        piece = lax.dot_general(table, pair, (((1,), (1,)), ((), ())), preferred_element_type=F32)
-        out_ref[d] = piece.astype(BF)
+        first, second = low_ref[route_ref[0, d]], high_ref[route_ref[1, d]]
+        out_ref[d] = jnp.where(upper, second, first).astype(BF)
         return 0
 
     lax.fori_loop(0, out_ref.shape[0], step, 0, unroll=8)
@@ -234,23 +274,18 @@
     down_ref[width : width + half] = pooled_ref[height // 2 - 1].astype(BF)
 
 
-def head_back_kernel(pooled_ref, up_ref, down_ref, edge_ref, weights_ref, grad_ref, rows3):
+def head_back_kernel(pooled_ref, up_ref, down_ref, edge_ref, weights_ref, grad_ref, rows3, table):
     height, width, chans = pooled_ref.shape
     start = up_ref.shape[0] - width
+    build_table(table, weights_ref, True)
     put_row(rows3, 0, up_ref[start:].astype(F32) * edge_ref[0:1])
     put_row(rows3, height + 1, down_ref[start:].astype(F32) * edge_ref[1:2])
-
-    def fill(r, _):
-        put_row(rows3, r + 1, pooled_ref[r])
-        return 0
-
-    lax.fori_loop(0, height, fill, 0)
 
     def emit(r, value, carry):
         grad_ref[r] = value
         return carry
 
-    conv_pairs(rows3, weights_ref, height, emit, 0)
+    conv_pairs(rows3, table, height, lambda r: put_row(rows3, r, pooled_ref[r - 1]), emit, 0)
 
 
 def hidden_kernel(route_ref, arrived_ref, noisy_ref, lift_ref, hid_ref, cond_ref, up_ref, down_ref,
@@ -287,28 +322,28 @@
     act_ref[0] = above.astype(BF)
     act_ref[height + 1] = below.astype(BF)
 
-    def fill(r, _):
-        value = act_of(x_ref[r], vec)
-        put_row(rows3, r + 1, value)
-        act_ref[r + 1] = value.astype(BF)
-        return 0
-
-    lax.fori_loop(0, height, fill, 0)
+    def fill(r):
+        value = act_of(x_ref[r - 1], vec)
+        put_row(rows3, r, value)
+        act_ref[r] = value.astype(BF)
+
+    return fill
 
 
 def make_first(count):
     def kernel(x_ref, up_ref, down_ref, opp_ref, own_ref, edge_ref, gain_ref, weights_ref,
-               y_ref, act_ref, vec_ref, to_up, to_down, block_ref, rows3):
+               y_ref, act_ref, vec_ref, to_up, to_down, block_ref, rows3, table):
         height, width, chans = x_ref.shape
         vec = norm_vectors(up_ref, down_ref, opp_ref, own_ref, gain_ref, width, height, count)
         vec_ref[...] = vec
-        norm_rows(x_ref, vec, up_ref, down_ref, edge_ref, rows3, act_ref)
+        build_table(table, weights_ref, False)
+        fill = norm_rows(x_ref, vec, up_ref, down_ref, edge_ref, rows3, act_ref)
 
         def emit(r, value, sums):
             y_ref[r] = value
             return add_sums(sums, value)
 
-        sums = conv_pairs(rows3, weights_ref, height, emit, zeros2(chans))
+        sums = conv_pairs(rows3, table, height, fill, emit, zeros2(chans))
         send_raw(to_up, to_down, block_ref, y_ref[0], y_ref[height - 1], sums, width, height)
 
     return kernel
@@ -316,27 +351,26 @@
 
 def make_second(count):
     def kernel(y_ref, up_ref, down_ref, opp_ref, own_ref, edge_ref, gain_ref, weights_ref, hid_ref,
-               level_ref, pooled_ref, act_ref, vec_ref, to_up, to_down, block_ref, rows3, line_ref):
+               level_ref, pooled_ref, act_ref, vec_ref, to_up, to_down, block_ref, rows3, table,
+               line_ref):
         height, width, chans = y_ref.shape
         half = width // 2
         vec = norm_vectors(up_ref, down_ref, opp_ref, own_ref, gain_ref, width, height, count)
         vec_ref[...] = vec
-        norm_rows(y_ref, vec, up_ref, down_ref, edge_ref, rows3, act_ref)
-        table = weights_ref[...]
-
-        def step(j, sums):
-            lhs = jnp.concatenate([rows3[2 * j + s] for s in range(SPAN)], axis=1)
-            out = jnp.dot(lhs, table, preferred_element_type=F32)
-            one = hid_ref[2 * j] + out[:, :chans]
-            two = hid_ref[2 * j + 1] + out[:, chans:]
-            level_ref[2 * j] = one
-            level_ref[2 * j + 1] = two
-            line_ref[...] = one + two
+        build_table(table, weights_ref, False)
+        fill = norm_rows(y_ref, vec, up_ref, down_ref, edge_ref, rows3, act_ref)
+
+        def emit(r, value, carry):
+            one = hid_ref[r] + value
+            level_ref[r] = one
+            if carry[0] is None:
+                return one, carry[1]
+            line_ref[...] = carry[0] + one
             pooled = 0.25 * (line_ref[pl.ds(0, half, stride=2)] + line_ref[pl.ds(1, half, stride=2)])
-            pooled_ref[j] = pooled
-            return add_sums(sums, pooled)
-
-        sums = lax.fori_loop(0, height // 2, step, zeros2(chans))
+            pooled_ref[r // 2] = pooled
+            return None, add_sums(carry[1], pooled)
+
+        sums = conv_pairs(rows3, table, height, fill, emit, (None, zeros2(chans)))[1]
         last = height // 2 - 1
         send_raw(to_up, to_down, block_ref, pooled_ref[0], pooled_ref[last], sums, half, height // 2)
 
@@ -367,14 +401,11 @@
     return kernel
 
 
-def tail_kernel(act_ref, weights_ref, pooled_ref, level_ref, out_ref, rows3, line_ref):
+def tail_kernel(act_ref, weights_ref, pooled_ref, level_ref, out_ref, rows3, table, line_ref):
     height, width, chans = pooled_ref.shape
-
-    def fill(r, _):
-        put_row(rows3, r, act_ref[r].astype(F32))
-        return 0
-
-    lax.fori_loop(0, height + 2, fill, 0)
+    build_table(table, weights_ref, False)
+    put_row(rows3, 0, act_ref[0].astype(F32))
+    put_row(rows3, height + 1, act_ref[height + 1].astype(F32))
 
     def emit(r, value, carry):
         two = pooled_ref[r] + value
@@ -385,10 +416,10 @@
         out_ref[2 * r + 1] = level_ref[2 * r + 1] + wide
         return carry
 
-    conv_pairs(rows3, weights_ref, height, emit, 0)
-
-
-def back_conv(rows3, weights_ref, x_ref, vec, grad_ref, to_up, to_down, block_ref):
+    conv_pairs(rows3, table, height, lambda r: put_row(rows3, r, act_ref[r].astype(F32)), emit, 0)
+
+
+def back_conv(rows3, table, fill, x_ref, vec, grad_ref, to_up, to_down, block_ref):
     height, width, chans = x_ref.shape
 
     def emit(r, value, sums):
@@ -396,14 +427,14 @@
         gs, normed = act_grad(value, x_ref[r], vec)
         return sums[0] + fold8(gs), sums[1] + fold8(gs * normed)
 
-    sums = conv_pairs(rows3, weights_ref, height, emit, zeros2(chans))
+    sums = conv_pairs(rows3, table, height, fill, emit, zeros2(chans))
     send_grad(to_up, to_down, block_ref, grad_ref[0], grad_ref[height - 1], sums, width)
 
 
 def make_back_mid(count):
     def kernel(ga_ref, y_ref, yup_ref, ydown_ref, vec_ref, gup_ref, gdown_ref, opp_ref, own_ref,
                edge_ref, weights_ref, x_ref, xvec_ref,
-               g_ref, out_ref, to_up, to_down, block_ref, rows3):
+               g_ref, out_ref, to_up, to_down, block_ref, rows3, table):
         height, width, chans = y_ref.shape
         vec = vec_ref[...]
         first, second = back_vectors(gup_ref, gdown_ref, opp_ref, own_ref, vec, width, count)
@@ -413,14 +444,13 @@
         put_row(rows3, 0, g_above * edge_ref[0:1])
         put_row(rows3, height + 1, g_below * edge_ref[1:2])
 
-        def fill(r, _):
-            value = norm_grad(ga_ref[r], y_ref[r], vec, first, second)
-            put_row(rows3, r + 1, value)
-            g_ref[r] = value.astype(BF)
-            return 0
-
-        lax.fori_loop(0, height, fill, 0)
-        back_conv(rows3, weights_ref, x_ref, xvec_ref[...], out_ref, to_up, to_down, block_ref)
+        def fill(r):
+            value = norm_grad(ga_ref[r - 1], y_ref[r - 1], vec, first, second)
+            put_row(rows3, r, value)
+            g_ref[r - 1] = value.astype(BF)
+
+        build_table(table, weights_ref, True)
+        back_conv(rows3, table, fill, x_ref, xvec_ref[...], out_ref, to_up, to_down, block_ref)
 
     return kernel
 
@@ -428,7 +458,7 @@
 def make_back_join(count):
     def kernel(ga_ref, p_ref, pup_ref, pdown_ref, pvec_ref, gup_ref, gdown_ref, opp_ref, own_ref,
                edge_ref, pg_ref, og_ref, oup_ref, odown_ref, weights_ref, x_ref, xvec_ref,
-               level_ref, g_ref, out_ref, to_up, to_down, block_ref, rows3, line_ref):
+               level_ref, g_ref, out_ref, to_up, to_down, block_ref, rows3, table, line_ref):
         half_height, half, chans = p_ref.shape
         height, width, _ = og_ref.shape
         vec = pvec_ref[...]
@@ -447,18 +477,22 @@
         wide = widened(g_below + odown_ref[width : width + half].astype(F32))
         put_row(rows3, height + 1, (odown_ref[0:width].astype(F32) + wide) * edge_ref[1:2])
 
-        def fill(r, _):
+        def widen_row(r, _):
             value = pg_ref[r] + norm_grad(ga_ref[r], p_ref[r], vec, first, second)
             wide = widened(value)
             for i in range(2):
                 grad = og_ref[2 * r + i] + wide
                 level_ref[2 * r + i] = grad
-                put_row(rows3, 2 * r + i + 1, grad)
-                g_ref[2 * r + i] = grad.astype(BF)
             return 0
 
-        lax.fori_loop(0, half_height, fill, 0)
-        back_conv(rows3, weights_ref, x_ref, xvec_ref[...], out_ref, to_up, to_down, block_ref)
+        def fill(r):
+            grad = level_ref[r - 1]
+            put_row(rows3, r, grad)
+            g_ref[r - 1] = grad.astype(BF)
+
+        build_table(table, weights_ref, True)
+        lax.fori_loop(0, half_height, widen_row, 0)
+        back_conv(rows3, table, fill, x_ref, xvec_ref[...], out_ref, to_up, to_down, block_ref)
 
     return kernel
 
@@ -550,14 +584,28 @@
     interp_out[...] = jnp.zeros(interp_out.shape, F32)
 
     def finish(b, _):
-        total = sums_ref[b].astype(BF)
+        one, two = sums_ref[2 * b], sums_ref[2 * b + 1]
+        one, two = one + pltpu.roll(one, half, 1), two + pltpu.roll(two, half, 1)
+        total = jnp.where(upper, two, one).astype(BF)
         wide = lax.dot_general(total, table, (((0,), (0,)), ((), ())), preferred_element_type=F32)
-        grad_ref[b] = wide[:half] + wide[half:]
-        pair = jnp.concatenate([coarse_ref[b], coarse_ref[b]], axis=0)
+        grad_ref[pl.ds(2 * b, 2)] = wide.reshape(2, half, wide.shape[1])
+        pair = coarse_ref[pl.ds(2 * b, 2)].reshape(lanes, coarse_ref.shape[2])
         interp_out[...] += jnp.dot(total, pair, preferred_element_type=F32)
         return 0
 
-    lax.fori_loop(0, blocks, finish, 0, unroll=4)
+    lax.fori_loop(0, blocks // 2, finish, 0, unroll=4)
+
+
+def finish_kernel(sums_ref, conv_ref, extra_ref, interp_ref):
+    devices, rows, lanes = sums_ref.shape
+    taps = conv_ref.shape[0] // devices
+    region = interp_ref.shape[0]
+    for d in range(devices):
+        part = sums_ref[d].astype(F32)
+        conv_ref[d * taps : (d + 1) * taps] = part[0:taps]
+        extra_ref[d : d + 1] = part[taps : taps + 1]
+        if d < region:
+            interp_ref[d : d + 1] = part[taps + 1 : taps + 2]
 
 
 def ring(x, shift):
@@ -569,13 +617,8 @@
     return ring(to_down, 1), ring(to_up, -1), ring(block, 2), block
 
 
-def pair_weights(taps):
-    inner, outer = taps.shape[1], taps.shape[2]
-    rows = taps.reshape(3, 3 * inner, outer)
-    none = jnp.zeros((3 * inner, outer), taps.dtype)
-    one = jnp.concatenate([rows[0], rows[1], rows[2], none], axis=0)
-    two = jnp.concatenate([none, rows[0], rows[1], rows[2]], axis=0)
-    return jnp.concatenate([one, two], axis=1)
+def both(first, second):
+    return lax.optimization_barrier((first, second))
 
 
 def body(coarse, slot_owner, slot_block, interp, lift, conv_weights, gains, fine_noisy, out_grad):
@@ -595,28 +638,24 @@
 
     edge = jnp.stack([lat > 0, lat < lat_count - 1]).astype(F32)
     edge = jnp.broadcast_to(edge[:, None], (2, chans))
-    forward = [pair_weights(jnp.transpose(conv_weights[i], (0, 2, 1))) for i in range(4)]
-    backward = [pair_weights(conv_weights[i][::-1]) for i in range(4)]
+    turned = jnp.transpose(conv_weights, (0, 1, 3, 2))
+    forward = [turned[i] for i in range(4)]
+    backward = [conv_weights[i] for i in range(4)]
     lift_rows = jnp.concatenate([lift.T, lift.T], axis=0)
     lift_cols = jnp.concatenate([lift, lift], axis=1)
     gain_rows = [gains[i : i + 1] for i in range(4)]
 
     full = (height, width, chans)
     small = (half_height, half, chans)
-    full3 = ((height + 2, width, 3 * chans), BF)
-    small3 = ((half_height + 2, half, 3 * chans), BF)
+    table = ((SPAN * 3 * chans, 2 * chans), BF)
+    full3 = [((height + 2, width, 3 * chans), BF), table]
+    small3 = [((half_height + 2, half, 3 * chans), BF), table]
     line = ((width, chans), F32)
     vec_shape = ((8, chans), F32)
     full_act = ((height + 2, width, chans), BF)
     small_act = ((half_height + 2, half, chans), BF)
     full_msg = [((width + STAT_ROWS, chans), BF)] * 2 + [((STAT_ROWS, chans), BF)]
     small_msg = [((half + STAT_ROWS, chans), BF)] * 2 + [((STAT_ROWS, chans), BF)]
-
-    edge_msg = ((width + half, chans), BF)
-    pooled_grad, edge_up, edge_down = call(
-        pool_kernel, [(small, F32), edge_msg, edge_msg], [line], [], [grad], "pool_grad"
-    )
-    grad_above, grad_below = ring(edge_down, 1), ring(edge_up, -1)
 
     (route,) = call(
         route_kernel,
@@ -626,33 +665,41 @@
         [slot_owner[:, :, 0].T, slot_block.T],
         "route",
     )
+    piece_shape = (region, 2 * coarse_chans)
     (outgoing,) = call(
-        send_kernel, [((devices, region, 2 * coarse_chans), BF)], [], [route], [coarse, interp.T], "send"
-    )
-    outgoing, grad_above, grad_below = lax.optimization_barrier((outgoing, grad_above, grad_below))
+        send_kernel, [((devices,) + piece_shape, BF)], [((blocks,) + piece_shape, F32)] * 2, [route],
+        [coarse, interp.T], "send",
+    )
     arrived = lax.all_to_all(outgoing, BOTH, split_axis=0, concat_axis=0, tiled=True)
-    (act_grad_d,) = call(
-        head_back_kernel, [(small, F32)], [small3], [],
-        [pooled_grad, grad_above, grad_below, edge, backward[3]], "back_d",
-    )
+    edge_msg = ((width + half, chans), BF)
+    pooled_grad, edge_up, edge_down = call(
+        pool_kernel, [(small, F32), edge_msg, edge_msg], [line], [], [grad], "pool_grad"
+    )
+    grad_above, grad_below = ring(edge_down, 1), ring(edge_up, -1)
+    arrived, (pooled_grad, turned) = both(arrived, (pooled_grad, turned))
 
     hidden, cond, *msg = call(
         hidden_kernel, [(full, F32), (full, BF)] + full_msg, [line], [route],
         [arrived, noisy, lift_rows], "hidden",
     )
     msg_h = exchange(*msg)
+    (act_grad_d,) = call(
+        head_back_kernel, [(small, F32)], small3, [],
+        [pooled_grad, grad_above, grad_below, edge, backward[3]], "back_d",
+    )
+    msg_h, act_grad_d = both(msg_h, act_grad_d)
     conv_a, act_a, vec_a, *msg = call(
-        make_first(full_count), [(full, F32), full_act, vec_shape] + full_msg, [full3], [],
+        make_first(full_count), [(full, F32), full_act, vec_shape] + full_msg, full3, [],
         [hidden, *msg_h, edge, gain_rows[0], forward[0]], "conv_a",
     )
     msg_a = exchange(*msg)
     level, pooled, act_b, vec_b, *msg = call(
         make_second(full_count), [(full, F32), (small, F32), full_act, vec_shape] + small_msg,
-        [full3, line], [], [conv_a, *msg_a, edge, gain_rows[1], forward[1], hidden], "conv_b",
+        full3 + [line], [], [conv_a, *msg_a, edge, gain_rows[1], forward[1], hidden], "conv_b",
     )
     msg_p = exchange(*msg)
     conv_c, act_c, vec_c, *msg = call(
-        make_first(half_count), [(small, F32), small_act, vec_shape] + small_msg, [small3], [],
+        make_first(half_count), [(small, F32), small_act, vec_shape] + small_msg, small3, [],
         [pooled, *msg_p, edge, gain_rows[2], forward[2]], "conv_c",
     )
     msg_c = exchange(*msg)
@@ -661,40 +708,37 @@
         [conv_c, *msg_c, edge, gain_rows[3], act_grad_d], "turn_d",
     )
     back_d = exchange(*msg)
-    (denoised,) = call(
-        tail_kernel, [(full, F32)], [small3, line], [], [act_d, forward[3], pooled, level], "conv_d"
-    )
 
     def taps_grad(g, act, name):
-        rows3 = full3 if g.shape[1] == width else small3
+        rows3 = full3[0] if g.shape[1] == width else small3[0]
         acc = ((chans, 9 * chans), F32)
         return call(kernel_grad_kernel, [((9, chans, chans), BF)], [rows3, acc], [], [g, act], name)[0]
 
     taps_d = taps_grad(pooled_grad.astype(BF), act_d, "taps_d")
+    back_d, taps_d = both(back_d, taps_d)
     g_c, act_grad_c, *msg = call(
-        make_back_mid(half_count), [(small, BF), (small, F32)] + small_msg, [small3], [],
+        make_back_mid(half_count), [(small, BF), (small, F32)] + small_msg, small3, [],
         [act_grad_d, conv_c, msg_c[0], msg_c[1], vec_d, *back_d, edge, backward[2], pooled, vec_c],
         "back_c",
     )
     back_c = exchange(*msg)
     taps_c = taps_grad(g_c, act_c, "taps_c")
+    back_c, taps_c = both(back_c, taps_c)
     grad_level, g_b, act_grad_b, *msg = call(
         make_back_join(half_count), [(full, F32), (full, BF), (full, F32)] + full_msg,
-        [full3, line], [],
+        full3 + [line], [],
         [act_grad_c, pooled, msg_p[0], msg_p[1], vec_c, *back_c, edge, pooled_grad, grad,
          grad_above, grad_below, backward[1], conv_a, vec_b],
         "back_b",
     )
     back_b = exchange(*msg)
-    taps_b = taps_grad(g_b, act_b, "taps_b")
     g_a, act_grad_a, *msg = call(
-        make_back_mid(full_count), [(full, BF), (full, F32)] + full_msg, [full3], [],
+        make_back_mid(full_count), [(full, BF), (full, F32)] + full_msg, full3, [],
         [act_grad_b, conv_a, msg_a[0], msg_a[1], vec_b, *back_b, edge, backward[0], hidden, vec_a],
         "back_a",
     )
     block = msg[2]
     back_a = (ring(block, 1), ring(block, -1), ring(block, 2), block)
-    taps_a = taps_grad(g_a, act_a, "taps_a")
     placed, lift_term = call(
         make_last(full_count),
         [((devices, region, 2 * coarse_chans), BF), ((chans, 2 * coarse_chans), F32)], [line],
@@ -702,40 +746,55 @@
         [act_grad_a, hidden, vec_a, *back_a, grad_level, lift_cols, cond], "grad_pieces",
     )
 
+    placed, (g_a, g_b, act_d) = both(placed, (g_a, g_b, act_d))
+    returned = lax.all_to_all(placed, BOTH, split_axis=0, concat_axis=0, tiled=True)
+    taps_b = taps_grad(g_b, act_b, "taps_b")
+    taps_a = taps_grad(g_a, act_a, "taps_a")
+    (denoised,) = call(
+        tail_kernel, [(full, F32)], small3 + [line], [], [act_d, forward[3], pooled, level], "conv_d"
+    )
     gain_terms = jnp.concatenate(
-        [sum(stat_pair(m[3])[1:]) for m in (back_a, back_b, back_c, back_d)], axis=0
+        [stat_pair(m[3])[1] for m in (back_a, back_b, back_c, back_d)], axis=0
     )
     lift_sum = lift_term[:, :coarse_chans] + lift_term[:, coarse_chans:]
-    param_rows = chans * chans * 36 // (devices * chans)
+    param_rows = 36
+    lift_count = lift_sum.size // chans
     taps = jnp.concatenate(
         [t.reshape(-1, chans) for t in (taps_a, taps_b, taps_c, taps_d)]
     ).reshape(devices, param_rows, chans)
     extra = jnp.concatenate(
-        [lift_sum.reshape(-1, chans), gain_terms,
-         jnp.zeros((devices - lift_sum.size // chans - 4, chans), F32)]
+        [lift_sum.reshape(-1, chans), gain_terms, jnp.zeros((devices - lift_count - 4, chans), F32)]
     ).astype(BF).reshape(devices, 1, chans)
-    params = jnp.concatenate([taps, extra], axis=1)
-    returned = lax.all_to_all(placed, BOTH, split_axis=0, concat_axis=0, tiled=True)
+    params = jnp.concatenate([taps, extra, jnp.zeros((devices, 3, chans), BF)], axis=1)
+    returned, (params, denoised) = both(returned, (params, denoised))
     params = lax.all_to_all(params, BOTH, split_axis=0, concat_axis=0, tiled=True)
     coarse_grad, interp_term = call(
         owner_kernel, [((blocks, coarse_chans, cells), F32), ((region, cells), F32)],
-        [((blocks, region, 2 * coarse_chans), F32)], [route], [returned, coarse, interp.T], "owner",
+        [((blocks,) + piece_shape, F32)], [route], [returned, coarse, interp.T], "owner",
     )
     param_sum = jnp.sum(params.astype(F32), axis=0)
+    interp_term, param_sum = both(interp_term, param_sum)
     interp_rows = jnp.concatenate([interp_term, jnp.zeros((devices - region, cells), F32)])
     interp_parts = lax.all_to_all(
         interp_rows.astype(BF).reshape(devices, 1, cells), BOTH, split_axis=0, concat_axis=0, tiled=True
     )
+    scale = 1.0 / math.sqrt(height * width * devices)
     interp_sum = jnp.sum(interp_parts.astype(F32), axis=0)
-    scale = 1.0 / math.sqrt(height * width * devices)
-    chunk = jnp.concatenate([param_sum, interp_sum], axis=0) * scale
-    everything = lax.all_gather(chunk.astype(BF), BOTH).astype(F32)
-    conv_total = everything[:, :param_rows].reshape(4, 9, chans, chans)
-    extra_total = everything[:, param_rows]
-    lift_count = lift_sum.size // chans
+    row = lax.broadcasted_iota(jnp.int32, param_sum.shape, 0)
+    chunk = (jnp.where(row == param_rows + 1, interp_sum, param_sum) * scale).astype(BF)
+    everything = lax.all_to_all(
+        jnp.broadcast_to(chunk[None], (devices,) + chunk.shape), BOTH, split_axis=0, concat_axis=0,
+        tiled=True,
+    )
+    conv_total, extra_total, interp_total = call(
+        finish_kernel, [((devices * param_rows, chans), F32), ((devices, chans), F32),
+                        ((region, cells), F32)],
+        [], [], [everything], "finish",
+    )
+    conv_total = conv_total.reshape(4, 9, chans, chans)
     lift_total = extra_total[:lift_count].reshape(lift_sum.shape)
     gain_total = extra_total[lift_count : lift_count + 4]
-    interp_total = everything[:region, param_rows + 1].T
+    interp_total = interp_total.T
     return (
         jnp.transpose(denoised, (2, 0, 1))[None],
         coarse_grad,

time: 395 us -> 299 us (0.76)
  waiting for transfers between devices: 125 us -> 57.7 us
  Pallas kernels: 138 us -> 85.1 us
  blocking collectives: 0 us -> 26.3 us
  local copies, waits for them, and re-layouts: 30.9 us -> 45.1 us
  between operations: 14.8 us -> 1.29 us
  other arithmetic: 22.1 us -> 9.84 us
  starting transfers between devices: 62.4 us -> 72.1 us
    all_gather x1 -> x0, waiting for transfers between devices: 54.6 us -> none  [body(): everything = lax.all_gather(chunk.astype(BF), BOTH).astype(F32)]
    pallas_call x19 -> x20, Pallas kernels: 138 us -> 85.1 us  [call(): pl.pallas_call(kernel, out_shape=[jax.ShapeDtypeStruct(s, d) for s, d in...]
    unnamed x117 -> x118, local copies, waits for them, and re-layouts: 7.35 us -> 38.2 us
    all_to_all x0 -> x1, blocking collectives: none -> 26.3 us  [body(): lax.all_to_all(jnp.broadcast_to(chunk[None], (devices,) + chunk.shape), B...]
    all_to_all x1, waiting for transfers between devices: 22.5 us -> 0.01 us  [body(): lax.all_to_all(placed, BOTH, split_axis=0, concat_axis=0, tiled=True)]
    concatenate x5 -> x1, other arithmetic: 16.7 us -> 1.5 us  [body(): jnp.concatenate([taps, extra, jnp.zeros((devices, 3, chans), BF)], axis=1)]
    slice x29 -> x0, local copies, waits for them, and re-layouts: 14.2 us -> none  [the longest x27 10.6 us: pair_weights(): one = jnp.concatenate([rows[0], rows[1], rows[2], none], axis=0)]
    all_to_all x1, starting transfers between devices: 4.68 us -> 10.3 us  [body(): lax.all_to_all(params, BOTH, split_axis=0, concat_axis=0, tiled=True)]
  transfers between devices with their start and end apart: 31 -> 30, of which waited for: 10 -> 10; matrix products, arithmetic and copies ran while one was open for 9% -> 6% of each run, Pallas kernels for 12% -> 12%
where the time goes in v2:
time: 299 us; the launch traced here: 297 us
  Pallas kernels  85.1 us (28%)
  starting transfers between devices  72.1 us (24%)
  waiting for transfers between devices  57.7 us (19%)
  local copies, waits for them, and re-layouts  45.1 us (15%)
  blocking collectives  26.3 us (9%)
  other arithmetic  9.84 us (3%)
    pallas_call x20, Pallas kernels, call(): pl.pallas_call(kernel, out_shape=[jax.ShapeDtypeStruct(s, d) for s, d in...  85.1 us
    unnamed x118, local copies, waits for them, and re-layouts  38.2 us
    ppermute x26, starting transfers between devices, ring(): lax.ppermute(x, 'lat', [(i, (i + shift) % count) for i in range(count)])  27.7 us
    all_to_all x1, blocking collectives, body(): lax.all_to_all(jnp.broadcast_to(chunk[None], (devices,) + chunk.shape), B...  26.3 us
    all_to_all x1, waiting for transfers between devices, body(): lax.all_to_all(outgoing, BOTH, split_axis=0, concat_axis=0, tiled=True)  18.8 us
    all_to_all x1, starting transfers between devices, body(): lax.all_to_all(placed, BOTH, split_axis=0, concat_axis=0, tiled=True)  17.5 us
    ppermute x26, waiting for transfers between devices, ring(): lax.ppermute(x, 'lat', [(i, (i + shift) % count) for i in range(count)])  15.5 us
    all_to_all x1, waiting for transfers between devices, body(): lax.all_to_all(params, BOTH, split_axis=0, concat_axis=0, tiled=True)  13.9 us
  transfers between devices with their start and end apart: 30, of which 10 were waited for; matrix products, arithmetic and copies ran while one was open for 6% of the time, Pallas kernels for 12%

profile of v2, /device:TPU:1, one launch (start us, length us, event | category | flops | bytes accessed | tf_op | source)
XLA Modules:
  0.0 297.5 jit_solution(9820000034208709239)
XLA Ops:
  4.4 3.3 %send.1 = bf16[128,56,128]{2,1,0:T(8,128)(2,1)S(1)} custom-call(s32[8,128]{1,0:T(8,128)S(1)} %route.1.route_ref, bf16[64,64,128]{2,1,0:T(8,128)(2,1)S(1)} %copy-done.10, bf16[56,128]{1,0:T(8,128)(2,1)S(1)} %bitcast.66), custom_call_target="tpu_custom_call" | custom-call | tf_op jit(solution)/shard_map/send/pallas_call | solution.py:23
  8.9 11.9 %all-to-all-start = ((bf16[128,56,128]{2,1,0:T(8,128)(2,1)}), bf16[128,56,128]{2,1,0:T(8,128)(2,1)}, u32[]{:S(2)}, u32[]{:S(2)}) async-start(bf16[128,56,128]{2,1,0:T(8,128)(2,1)} %copy-done.6), calls=%async_computation | async-start | bytes 3670016 | tf_op jit(solution)/shard_map/all_to_all | solution.py:673
  25.5 1.7 copy.29
  29.2 18.8 %all-to-all-done.arrived_ref = bf16[128,56,128]{2,1,0:T(8,128)(2,1)} async-done(((bf16[128,56,128]{2,1,0:T(8,128)(2,1)}), bf16[128,56,128]{2,1,0:T(8,128)(2,1)}, u32[]{:S(2)}, u32[]{:S(2)}) %all-to-all-start) | async-done | bytes 1835040 | tf_op jit(solution)/shard_map/all_to_all | solution.py:673
  49.4 5.1 %hidden.1 = (f32[14,448,128]{2,1,0:T(8,128)S(1)}, bf16[14,448,128]{2,1,0:T(8,128)(2,1)S(1)}, bf16[464,128]{1,0:T(8,128)(2,1)}, bf16[464,128]{1,0:T(8,128)(2,1)}, bf16[16,128]{1,0:T(8,128)(2,1)S(1)}) custom-call(s32[8,128]{1,0:T(8,128)S(1)} %route.1.route_ref, bf16[128,56,128]{2,1,0:T(8,128)(2,1)} %all-to-all-done.arrived_ref, ...), custom_call_target="tpu_custom_call" | custom-call | tf_op jit(solution)/shard_map/hidden/pallas_call | solution.py:23
  56.0 2.4 collective-permute-start.1
  60.7 2.4 back_d.1.grad_ref.ga_ref
  63.2 7.2 %conv_a.1 = (f32[14,448,128]{2,1,0:T(8,128)S(1)}, bf16[16,448,128]{2,1,0:T(8,128)(2,1)S(1)}, f32[8,128]{1,0:T(8,128)S(1)}, bf16[464,128]{1,0:T(8,128)(2,1)S(1)},...) custom-call(f32[14,448,128]{2,1,0:T(8,128)S(1)} %get-tuple-element.94.x_ref.hid_ref, ...), custom_call_target="tpu_custom_call" | custom-call | tf_op jit(solution)/shard_map/conv_a/pallas_call | solution.py:23
  72.4 2.0 collective-permute-start.6
  74.4 1.7 collective-permute-start.7
  76.1 2.3 collective-permute-done.7.opp_ref
  78.4 6.5 %conv_b.1 = (f32[14,448,128]{2,1,0:T(8,128)S(1)}, f32[7,224,128]{2,1,0:T(8,128)S(1)}, bf16[16,448,128]{2,1,0:T(8,128)(2,1)S(1)}, f32[8,128]{1,0:T(8,128)S(1)}, b...) custom-call(f32[14,448,128]{2,1,0:T(8,128)S(1)} %get-tuple-element.99.y_ref.x_ref, ...), custom_call_target="tpu_custom_call" | custom-call | tf_op jit(solution)/shard_map/conv_b/pallas_call | solution.py:23
  85.0 1.7 copy-done.12
  86.7 2.7 collective-permute-start.9
  89.9 3.4 %collective-permute-done.10.opp_ref = bf16[16,128]{1,0:T(8,128)(2,1)S(1)} collective-permute-done((bf16[16,128]{1,0:T(8,128)(2,1)S(1)}, bf16[16,128]{1,0:T(8,128)(2,1)S(1)}, u32[]{:S(2)}, u32[]{:S(2)}) %collective-permute-start.10) | collective-permute-done | bytes 4128 | tf_op jit(solution)/shard_map/ppermute | solution.py:613
  93.3 1.8 conv_c.1
  95.2 2.7 collective-permute-start.12
  97.9 4.0 %collective-permute-done.13.opp_ref = bf16[16,128]{1,0:T(8,128)(2,1)S(1)} collective-permute-done((bf16[16,128]{1,0:T(8,128)(2,1)S(1)}, bf16[16,128]{1,0:T(8,128)(2,1)S(1)}, u32[]{:S(2)}, u32[]{:S(2)}) %collective-permute-start.13) | collective-permute-done | bytes 4128 | tf_op jit(solution)/shard_map/ppermute | solution.py:613
  102.8 2.7 collective-permute-start.15
  105.5 2.3 taps_d.1
  109.4 2.2 back_c.1
  111.8 2.7 collective-permute-start.18
  115.3 2.3 taps_c.1
  118.4 8.6 %back_b.1 = (f32[14,448,128]{2,1,0:T(8,128)S(1)}, bf16[14,448,128]{2,1,0:T(8,128)(2,1)S(1)}, f32[14,448,128]{2,1,0:T(8,128)S(1)}, bf16[464,128]{1,0:T(8,128)(2,1...) custom-call(f32[7,224,128]{2,1,0:T(8,128)S(1)} %get-tuple-element.121.ga_ref, ...), custom_call_target="tpu_custom_call" | custom-call | tf_op jit(solution)/shard_map/back_b/pallas_call | solution.py:23
  127.1 1.7 copy-done.14
  128.8 1.8 copy-done.16
  131.7 2.7 collective-permute-start.21
  136.0 2.3 collective-permute-done.22.opp_ref
  138.3 1.9 copy-done.1
  140.2 1.9 copy-done.17
  144.9 10.9 %back_a.1 = (bf16[14,448,128]{2,1,0:T(8,128)(2,1)S(1)}, f32[14,448,128]{2,1,0:T(8,128)S(1)}, bf16[464,128]{1,0:T(8,128)(2,1)}, bf16[464,128]{1,0:T(8,128)(2,1)}, bf16[16,128]{1,0:T(8,128)(2,1)S(1)}) custom-call(f32[14,448,128]{2,1,0:T(8,128)S(1)} %copy-done.17, f32[14,448,128]{2,1,0:T(8,128)S(1)} %copy-done.1, bf16[464,128]{1,0:T(8,128)(2,1)S(1)} %copy-done.44, ...), custom_call_target="tpu_custom_call" | custom-call | tf_op jit(solution)/shard_map/back_a/pallas_call | solution.py:23
  156.9 2.7 collective-permute-start.24
  161.6 2.0 collective-permute-done.25.opp_ref
  163.6 6.0 %grad_pieces.1 = (bf16[128,56,128]{2,1,0:T(8,128)(2,1)S(1)}, f32[128,128]{1,0:T(8,128)S(1)}) custom-call(s32[8,128]{1,0:T(8,128)S(1)} %route.1.route_ref, f32[14,448,128]{2,1,0:T(8,128)S(1)} %get-tuple-element.137.ga_ref, f32[14,448,128]{2,1,0:T(8,128)S(1)} %get-tuple-element.94.x_ref.hid_ref, f32[8,128]{1,0:T(8,128)S(1)} %get-tuple-element.136.xvec_ref.vec_ref, ...), custom_call_target="tpu_custom_call" | custom-call | tf_op jit(solution)/shard_map/grad_pieces/pallas_call | solution.py:23
  171.5 17.5 %all-to-all-start.1 = ((bf16[128,56,128]{2,1,0:T(8,128)(2,1)}), bf16[128,56,128]{2,1,0:T(8,128)(2,1)S(1)}, u32[]{:S(2)}, u32[]{:S(2)}) async-start(bf16[128,56,128]{2,1,0:T(8,128)(2,1)} %copy-done.24), calls=%async_computation.1 | async-start | bytes 3670016 | tf_op jit(solution)/shard_map/all_to_all | solution.py:750
  191.9 6.3 %taps_a.1 = bf16[9,128,128]{2,1,0:T(8,128)(2,1)S(1)} custom-call(bf16[14,448,128]{2,1,0:T(8,128)(2,1)S(1)} %copy-done.30, bf16[16,448,128]{2,1,0:T(8,128)(2,1)S(1)} %copy-done.21), custom_call_target="tpu_custom_call" | custom-call | tf_op jit(solution)/shard_map/taps_a/pallas_call | solution.py:23
  198.3 6.4 %taps_b.1 = bf16[9,128,128]{2,1,0:T(8,128)(2,1)S(1)} custom-call(bf16[14,448,128]{2,1,0:T(8,128)(2,1)S(1)} %copy-done.28, bf16[16,448,128]{2,1,0:T(8,128)(2,1)S(1)} %copy-done.23), custom_call_target="tpu_custom_call" | custom-call | tf_op jit(solution)/shard_map/taps_b/pallas_call | solution.py:23
  205.8 3.1 %reshape.147 = bf16[128,36,128]{2,1,0:T(8,128)(2,1)} reshape(bf16[4608,128]{1,0:T(8,128)(2,1)} %pad_maximum_fusion) | data formatting | bytes 2359296 | tf_op jit(solution)/shard_map/reshape | solution.py:764
  210.1 1.9 copy-done.13
  212.0 3.5 %conv_d.1 = f32[14,448,128]{2,1,0:T(8,128)} custom-call(bf16[9,224,128]{2,1,0:T(8,128)(2,1)S(1)} %copy-done.19, bf16[9,128,128]{2,1,0:T(8,128)(2,1)S(1)} %get-tuple-element.182.weights_ref, f32[7,224,128]{2,1,0:T(8,128)S(1)} %copy-done.5, f32[14,448,128]{2,1,0:T(8,128)S(1)} %copy-done.13), custom_call_target="tpu_custom_call" | custom-call | tf_op jit(solution)/shard_map/conv_d/pallas_call | solution.py:23
  219.5 10.3 %all-to-all-start.2 = ((bf16[128,40,128]{2,1,0:T(8,128)(2,1)}), bf16[128,40,128]{2,1,0:T(8,128)(2,1)}, u32[]{:S(2)}, u32[]{:S(2)}) async-start(bf16[128,40,128]{2,1,0:T(8,128)(2,1)} %maximum_maximum_fusion), calls=%async_computation.2 | async-start | bytes 2621440 | tf_op jit(solution)/shard_map/all_to_all | solution.py:770
  231.0 6.4 %owner.1 = (f32[64,64,128]{2,1,0:T(8,128)}, f32[56,128]{1,0:T(8,128)S(1)}) custom-call(s32[8,128]{1,0:T(8,128)S(1)} %route.1.route_ref, bf16[128,56,128]{2,1,0:T(8,128)(2,1)S(1)} %all-to-all-done.1.arrived_ref, bf16[64,64,128]{2,1,0:T(8,128)(2,1)S(1)} %copy-done.11, bf16[56,128]{1,0:T(8,128)(2,1)S(1)} %bitcast.67), custom_call_target="tpu_custom_call" | custom-call | tf_op jit(solution)/shard_map/owner/pallas_call | solution.py:23
  237.5 13.9 %all-to-all-done.2 = bf16[128,40,128]{2,1,0:T(8,128)(2,1)} async-done(((bf16[128,40,128]{2,1,0:T(8,128)(2,1)}), bf16[128,40,128]{2,1,0:T(8,128)(2,1)}, u32[]{:S(2)}, u32[]{:S(2)}) %all-to-all-start.2) | async-done | bytes 1310752 | tf_op jit(solution)/shard_map/all_to_all | solution.py:770
  251.4 1.6 convert_reduce_fusion
  253.7 4.6 %all-to-all-start.3 = ((bf16[128,1,128]{2,1,0:T(2,128)(2,1)}), bf16[128,1,128]{2,1,0:T(2,128)(2,1)S(1)}, u32[]{:S(2)}, u32[]{:S(2)}) async-start(bf16[128,1,128]{2,1,0:T(2,128)(2,1)} %copy.33), calls=%async_computation.3 | async-start | bytes 131072 | tf_op jit(solution)/shard_map/all_to_all | solution.py:778
  258.3 9.5 %all-to-all-done.3 = bf16[128,1,128]{2,1,0:T(2,128)(2,1)S(1)} async-done(((bf16[128,1,128]{2,1,0:T(2,128)(2,1)}), bf16[128,1,128]{2,1,0:T(2,128)(2,1)S(1)}, u32[]{:S(2)}, u32[]{:S(2)}) %all-to-all-start.3) | async-done | bytes 32800 | tf_op jit(solution)/shard_map/all_to_all | solution.py:778
  268.2 26.3 %all_to_all.25.sums_ref = bf16[128,40,128]{2,1,0:T(8,128)(2,1)S(1)} all-to-all(bf16[128,40,128]{2,1,0:T(8,128)(2,1)S(1)} %broadcast_in_dim.35), channel_id=1, replica_groups=mesh['lat'=4,'patch'=32] {'lat','patch'}, dimensions={0} | all-to-all | bytes 2621440 | tf_op jit(solution)/shard_map/all_to_all | solution.py:785
  294.5 1.6 finish.1
  (186 shorter events, 47.0 us)
Async XLA Ops:
  8.9 11.9 %copy-start.2 = (f32[1,128,14,448]{1,3,2,0:T(8,128)S(1)}, f32[1,128,14,448]{1,3,2,0:T(8,128)}, u32[]{:S(2)}) copy-start(f32[1,128,14,448]{1,3,2,0:T(8,128)} %param.17) | copy-start | bytes 9633796
  8.9 39.1 %all-to-all-start = ((bf16[128,56,128]{2,1,0:T(8,128)(2,1)}), bf16[128,56,128]{2,1,0:T(8,128)(2,1)}, u32[]{:S(2)}, u32[]{:S(2)}) async-start(bf16[128,56,128]{2,1,0:T(8,128)(2,1)} %copy-done.6), calls=%async_computation | async-start | bytes 3670016 | tf_op jit(solution)/shard_map/all_to_all | solution.py:673
  22.8 35.7 %collective-permute-start.3 = (bf16[672,128]{1,0:T(8,128)(2,1)}, bf16[672,128]{1,0:T(8,128)(2,1)}, u32[]{:S(2)}, u32[]{:S(2)}) collective-permute-start(bf16[672,128]{1,0:T(8,128)(2,1)} %get-tuple-element.91), channel_id=1, source_target_pairs={{0,32},{32,64},{64,96},{96,0},{1,33},{33,65},{65,97},{97,1},{2,34}... | collective-permute-start | bytes 516104 | tf_op jit(solution)/shard_map/ppermute | solution.py:613
  24.2 34.3 %collective-permute-start.4 = (bf16[672,128]{1,0:T(8,128)(2,1)}, bf16[672,128]{1,0:T(8,128)(2,1)}, u32[]{:S(2)}, u32[]{:S(2)}) collective-permute-start(bf16[672,128]{1,0:T(8,128)(2,1)} %get-tuple-element.92), channel_id=1, source_target_pairs={{0,96},{32,0},{64,32},{96,64},{1,97},{33,1},{65,33},{97,65},{2,98}... | collective-permute-start | bytes 516104 | tf_op jit(solution)/shard_map/ppermute | solution.py:613
  29.2 29.2 %copy-start.56 = (f32[4,128]{1,0:T(4,128)S(1)}, f32[4,128]{1,0:T(4,128)}, u32[]{:S(2)}) copy-start(f32[4,128]{1,0:T(4,128)} %param.15) | copy-start | bytes 6148
  55.7 7.4 %collective-permute-start = (bf16[464,128]{1,0:T(8,128)(2,1)}, bf16[464,128]{1,0:T(8,128)(2,1)}, u32[]{:S(2)}, u32[]{:S(2)}) collective-permute-start(bf16[464,128]{1,0:T(8,128)(2,1)} %get-tuple-element.87), channel_id=1, source_target_pairs={{0,32},{32,64},{64,96},{96,0},{1,33},{33,65},{65,97},{97,1},{2,34}... | collective-permute-start | bytes 356360 | tf_op jit(solution)/shard_map/ppermute | solution.py:613
  56.0 7.1 %collective-permute-start.1 = (bf16[464,128]{1,0:T(8,128)(2,1)}, bf16[464,128]{1,0:T(8,128)(2,1)}, u32[]{:S(2)}, u32[]{:S(2)}) collective-permute-start(bf16[464,128]{1,0:T(8,128)(2,1)} %get-tuple-element.88), channel_id=1, source_target_pairs={{0,96},{32,0},{64,32},{96,64},{1,97},{33,1},{65,33},{97,65},{2,98}... | collective-permute-start | bytes 356360 | tf_op jit(solution)/shard_map/ppermute | solution.py:613
  58.4 4.7 %collective-permute-start.2 = (bf16[16,128]{1,0:T(8,128)(2,1)S(1)}, bf16[16,128]{1,0:T(8,128)(2,1)S(1)}, u32[]{:S(2)}, u32[]{:S(2)}) collective-permute-start(bf16[16,128]{1,0:T(8,128)(2,1)S(1)} %get-tuple-element.98.own_ref), channel_id=1, source_target_pairs={{0,64},{32,96},{64,0},{96,32},{1,65},{33,97},{65,1},{97,33},{2,66}... | collective-permute-start | bytes 12296 | tf_op jit(solution)/shard_map/ppermute | solution.py:613
  63.2 15.2 %copy-start.34 = (bf16[9,128,128]{2,1,0:T(8,128)(2,1)S(1)}, bf16[9,128,128]{2,1,0:T(8,128)(2,1)}, u32[]{:S(2)}) copy-start(bf16[9,128,128]{2,1,0:T(8,128)(2,1)} %get-tuple-element.184.weights_ref) | copy-start | bytes 884740
  71.7 46.7 %copy-start = (f32[14,448,128]{2,1,0:T(8,128)}, f32[14,448,128]{2,1,0:T(8,128)S(1)}, u32[]{:S(2)}) copy-start(f32[14,448,128]{2,1,0:T(8,128)S(1)} %get-tuple-element.99.y_ref.x_ref) | copy-start | bytes 9633796
  71.7 6.7 %collective-permute-start.5 = (bf16[464,128]{1,0:T(8,128)(2,1)S(1)}, bf16[464,128]{1,0:T(8,128)(2,1)S(1)}, u32[]{:S(2)}, u32[]{:S(2)}) collective-permute-start(bf16[464,128]{1,0:T(8,128)(2,1)S(1)} %get-tuple-element.100), channel_id=1, source_target_pairs={{0,32},{32,64},{64,96},{96,0},{1,33},{33,65},{65,97},{97,1},{2,34}... | collective-permute-start | bytes 356360 | tf_op jit(solution)/shard_map/ppermute | solution.py:613
  72.4 6.0 %collective-permute-start.6 = (bf16[464,128]{1,0:T(8,128)(2,1)S(1)}, bf16[464,128]{1,0:T(8,128)(2,1)S(1)}, u32[]{:S(2)}, u32[]{:S(2)}) collective-permute-start(bf16[464,128]{1,0:T(8,128)(2,1)S(1)} %get-tuple-element.101), channel_id=1, source_target_pairs={{0,96},{32,0},{64,32},{96,64},{1,97},{33,1},{65,33},{97,65},{2,98}... | collective-permute-start | bytes 356360 | tf_op jit(solution)/shard_map/ppermute | solution.py:613
  74.4 4.0 %collective-permute-start.7 = (bf16[16,128]{1,0:T(8,128)(2,1)S(1)}, bf16[16,128]{1,0:T(8,128)(2,1)S(1)}, u32[]{:S(2)}, u32[]{:S(2)}) collective-permute-start(bf16[16,128]{1,0:T(8,128)(2,1)S(1)} %get-tuple-element.102.own_ref), channel_id=1, source_target_pairs={{0,64},{32,96},{64,0},{96,32},{1,65},{33,97},{65,1},{97,33},{2,66}... | collective-permute-start | bytes 12296 | tf_op jit(solution)/shard_map/ppermute | solution.py:613
  78.4 6.5 %copy-start.45 = (bf16[464,128]{1,0:T(8,128)(2,1)}, bf16[464,128]{1,0:T(8,128)(2,1)S(1)}, u32[]{:S(2)}) copy-start(bf16[464,128]{1,0:T(8,128)(2,1)S(1)} %collective-permute-done.6.down_ref.ydown_ref) | copy-start | bytes 356356
  78.4 14.9 %copy-start.39 = (bf16[9,128,128]{2,1,0:T(8,128)(2,1)S(1)}, bf16[9,128,128]{2,1,0:T(8,128)(2,1)}, u32[]{:S(2)}) copy-start(bf16[9,128,128]{2,1,0:T(8,128)(2,1)} %get-tuple-element.183.weights_ref) | copy-start | bytes 884740
  86.6 18.9 %copy-start.22 = (bf16[16,448,128]{2,1,0:T(8,128)(2,1)}, bf16[16,448,128]{2,1,0:T(8,128)(2,1)S(1)}, u32[]{:S(2)}) copy-start(bf16[16,448,128]{2,1,0:T(8,128)(2,1)S(1)} %get-tuple-element.148.act_ref) | copy-start | bytes 5505028
  86.6 31.8 %copy-start.4 = (f32[7,224,128]{2,1,0:T(8,128)}, f32[7,224,128]{2,1,0:T(8,128)S(1)}, u32[]{:S(2)}) copy-start(f32[7,224,128]{2,1,0:T(8,128)S(1)} %get-tuple-element.103.x_ref.p_ref.pooled_ref) | copy-start | bytes 2408452
  86.6 18.8 %copy-start.9 = (f32[7,224,128]{2,1,0:T(8,128)S(1)}, f32[7,224,128]{2,1,0:T(8,128)}, u32[]{:S(2)}) copy-start(f32[7,224,128]{2,1,0:T(8,128)} %copy-done.7) | copy-start | bytes 2408452
  86.6 6.6 %collective-permute-start.8 = (bf16[240,128]{1,0:T(8,128)(2,1)S(1)}, bf16[240,128]{1,0:T(8,128)(2,1)S(1)}, u32[]{:S(2)}, u32[]{:S(2)}) collective-permute-start(bf16[240,128]{1,0:T(8,128)(2,1)S(1)} %get-tuple-element.104), channel_id=1, source_target_pairs={{0,32},{32,64},{64,96},{96,0},{1,33},{33,65},{65,97},{97,1},{2,34}... | collective-permute-start | bytes 184328 | tf_op jit(solution)/shard_map/ppermute | solution.py:613
  86.7 6.6 %collective-permute-start.9 = (bf16[240,128]{1,0:T(8,128)(2,1)S(1)}, bf16[240,128]{1,0:T(8,128)(2,1)S(1)}, u32[]{:S(2)}, u32[]{:S(2)}) collective-permute-start(bf16[240,128]{1,0:T(8,128)(2,1)S(1)} %get-tuple-element.105), channel_id=1, source_target_pairs={{0,96},{32,0},{64,32},{96,64},{1,97},{33,1},{65,33},{97,65},{2,98}... | collective-permute-start | bytes 184328 | tf_op jit(solution)/shard_map/ppermute | solution.py:613
  89.3 4.0 %collective-permute-start.10 = (bf16[16,128]{1,0:T(8,128)(2,1)S(1)}, bf16[16,128]{1,0:T(8,128)(2,1)S(1)}, u32[]{:S(2)}, u32[]{:S(2)}) collective-permute-start(bf16[16,128]{1,0:T(8,128)(2,1)S(1)} %get-tuple-element.106.own_ref), channel_id=1, source_target_pairs={{0,64},{32,96},{64,0},{96,32},{1,65},{33,97},{65,1},{97,33},{2,66}... | collective-permute-start | bytes 12296 | tf_op jit(solution)/shard_map/ppermute | solution.py:613
  95.1 6.7 %collective-permute-start.11 = (bf16[240,128]{1,0:T(8,128)(2,1)S(1)}, bf16[240,128]{1,0:T(8,128)(2,1)S(1)}, u32[]{:S(2)}, u32[]{:S(2)}) collective-permute-start(bf16[240,128]{1,0:T(8,128)(2,1)S(1)} %get-tuple-element.108), channel_id=1, source_target_pairs={{0,32},{32,64},{64,96},{96,0},{1,33},{33,65},{65,97},{97,1},{2,34}... | collective-permute-start | bytes 184328 | tf_op jit(solution)/shard_map/ppermute | solution.py:613
  95.2 6.6 %collective-permute-start.12 = (bf16[240,128]{1,0:T(8,128)(2,1)S(1)}, bf16[240,128]{1,0:T(8,128)(2,1)S(1)}, u32[]{:S(2)}, u32[]{:S(2)}) collective-permute-start(bf16[240,128]{1,0:T(8,128)(2,1)S(1)} %get-tuple-element.109), channel_id=1, source_target_pairs={{0,96},{32,0},{64,32},{96,64},{1,97},{33,1},{65,33},{97,65},{2,98}... | collective-permute-start | bytes 184328 | tf_op jit(solution)/shard_map/ppermute | solution.py:613
  97.9 4.0 %collective-permute-start.13 = (bf16[16,128]{1,0:T(8,128)(2,1)S(1)}, bf16[16,128]{1,0:T(8,128)(2,1)S(1)}, u32[]{:S(2)}, u32[]{:S(2)}) collective-permute-start(bf16[16,128]{1,0:T(8,128)(2,1)S(1)} %get-tuple-element.110.own_ref), channel_id=1, source_target_pairs={{0,64},{32,96},{64,0},{96,32},{1,65},{33,97},{65,1},{97,33},{2,66}... | collective-permute-start | bytes 12296 | tf_op jit(solution)/shard_map/ppermute | solution.py:613
  101.9 7.6 %copy-start.36 = (bf16[9,128,128]{2,1,0:T(8,128)(2,1)S(1)}, bf16[9,128,128]{2,1,0:T(8,128)(2,1)}, u32[]{:S(2)}) copy-start(bf16[9,128,128]{2,1,0:T(8,128)(2,1)} %get-tuple-element.187.weights_ref) | copy-start | bytes 884740
  102.7 9.0 %copy-start.18 = (bf16[9,224,128]{2,1,0:T(8,128)(2,1)}, bf16[9,224,128]{2,1,0:T(8,128)(2,1)S(1)}, u32[]{:S(2)}) copy-start(bf16[9,224,128]{2,1,0:T(8,128)(2,1)S(1)} %get-tuple-element.152.act_ref) | copy-start | bytes 1548292
  102.7 6.7 %collective-permute-start.14 = (bf16[240,128]{1,0:T(8,128)(2,1)S(1)}, bf16[240,128]{1,0:T(8,128)(2,1)S(1)}, u32[]{:S(2)}, u32[]{:S(2)}) collective-permute-start(bf16[240,128]{1,0:T(8,128)(2,1)S(1)} %get-tuple-element.112), channel_id=1, source_target_pairs={{0,32},{32,64},{64,96},{96,0},{1,33},{33,65},{65,97},{97,1},{2,34}... | collective-permute-start | bytes 184328 | tf_op jit(solution)/shard_map/ppermute | solution.py:613
  102.8 6.6 %collective-permute-start.15 = (bf16[240,128]{1,0:T(8,128)(2,1)S(1)}, bf16[240,128]{1,0:T(8,128)(2,1)S(1)}, u32[]{:S(2)}, u32[]{:S(2)}) collective-permute-start(bf16[240,128]{1,0:T(8,128)(2,1)S(1)} %get-tuple-element.113), channel_id=1, source_target_pairs={{0,96},{32,0},{64,32},{96,64},{1,97},{33,1},{65,33},{97,65},{2,98}... | collective-permute-start | bytes 184328 | tf_op jit(solution)/shard_map/ppermute | solution.py:613
  105.4 4.0 %collective-permute-start.16 = (bf16[16,128]{1,0:T(8,128)(2,1)S(1)}, bf16[16,128]{1,0:T(8,128)(2,1)S(1)}, u32[]{:S(2)}, u32[]{:S(2)}) collective-permute-start(bf16[16,128]{1,0:T(8,128)(2,1)S(1)} %get-tuple-element.119.own_ref), channel_id=1, source_target_pairs={{0,64},{32,96},{64,0},{96,32},{1,65},{33,97},{65,1},{97,33},{2,66}... | collective-permute-start | bytes 12296 | tf_op jit(solution)/shard_map/ppermute | solution.py:613
  109.4 9.0 %copy-start.3 = (f32[1,128,14,448]{1,3,2,0:T(8,128)S(1)}, f32[1,128,14,448]{1,3,2,0:T(8,128)}, u32[]{:S(2)}) copy-start(f32[1,128,14,448]{1,3,2,0:T(8,128)} %param.17) | copy-start | bytes 9633796
  109.4 9.0 %copy-start.33 = (bf16[9,128,128]{2,1,0:T(8,128)(2,1)S(1)}, bf16[9,128,128]{2,1,0:T(8,128)(2,1)}, u32[]{:S(2)}) copy-start(bf16[9,128,128]{2,1,0:T(8,128)(2,1)} %get-tuple-element.189.weights_ref) | copy-start | bytes 884740
  111.7 6.7 %collective-permute-start.17 = (bf16[240,128]{1,0:T(8,128)(2,1)S(1)}, bf16[240,128]{1,0:T(8,128)(2,1)S(1)}, u32[]{:S(2)}, u32[]{:S(2)}) collective-permute-start(bf16[240,128]{1,0:T(8,128)(2,1)S(1)} %get-tuple-element.122), channel_id=1, source_target_pairs={{0,32},{32,64},{64,96},{96,0},{1,33},{33,65},{65,97},{97,1},{2,34}... | collective-permute-start | bytes 184328 | tf_op jit(solution)/shard_map/ppermute | solution.py:613
  111.8 6.6 %collective-permute-start.18 = (bf16[240,128]{1,0:T(8,128)(2,1)S(1)}, bf16[240,128]{1,0:T(8,128)(2,1)S(1)}, u32[]{:S(2)}, u32[]{:S(2)}) collective-permute-start(bf16[240,128]{1,0:T(8,128)(2,1)S(1)} %get-tuple-element.123), channel_id=1, source_target_pairs={{0,96},{32,0},{64,32},{96,64},{1,97},{33,1},{65,33},{97,65},{2,98}... | collective-permute-start | bytes 184328 | tf_op jit(solution)/shard_map/ppermute | solution.py:613
  114.4 4.0 %collective-permute-start.19 = (bf16[16,128]{1,0:T(8,128)(2,1)S(1)}, bf16[16,128]{1,0:T(8,128)(2,1)S(1)}, u32[]{:S(2)}, u32[]{:S(2)}) collective-permute-start(bf16[16,128]{1,0:T(8,128)(2,1)S(1)} %get-tuple-element.130.own_ref), channel_id=1, source_target_pairs={{0,64},{32,96},{64,0},{96,32},{1,65},{33,97},{65,1},{97,33},{2,66}... | collective-permute-start | bytes 12296 | tf_op jit(solution)/shard_map/ppermute | solution.py:613
  117.7 9.4 %copy-start.40 = (bf16[9,128,128]{2,1,0:T(8,128)(2,1)}, bf16[9,128,128]{2,1,0:T(8,128)(2,1)S(1)}, u32[]{:S(2)}) copy-start(bf16[9,128,128]{2,1,0:T(8,128)(2,1)S(1)} %taps_c.1) | copy-start | bytes 884740
  131.7 6.6 %collective-permute-start.20 = (bf16[464,128]{1,0:T(8,128)(2,1)}, bf16[464,128]{1,0:T(8,128)(2,1)}, u32[]{:S(2)}, u32[]{:S(2)}) collective-permute-start(bf16[464,128]{1,0:T(8,128)(2,1)} %get-tuple-element.133), channel_id=1, source_target_pairs={{0,32},{32,64},{64,96},{96,0},{1,33},{33,65},{65,97},{97,1},{2,34}... | collective-permute-start | bytes 356360 | tf_op jit(solution)/shard_map/ppermute | solution.py:613
  131.7 6.6 %collective-permute-start.21 = (bf16[464,128]{1,0:T(8,128)(2,1)}, bf16[464,128]{1,0:T(8,128)(2,1)}, u32[]{:S(2)}, u32[]{:S(2)}) collective-permute-start(bf16[464,128]{1,0:T(8,128)(2,1)} %get-tuple-element.134), channel_id=1, source_target_pairs={{0,96},{32,0},{64,32},{96,64},{1,97},{33,1},{65,33},{97,65},{2,98}... | collective-permute-start | bytes 356360 | tf_op jit(solution)/shard_map/ppermute | solution.py:613
  134.3 4.0 %collective-permute-start.22 = (bf16[16,128]{1,0:T(8,128)(2,1)S(1)}, bf16[16,128]{1,0:T(8,128)(2,1)S(1)}, u32[]{:S(2)}, u32[]{:S(2)}) collective-permute-start(bf16[16,128]{1,0:T(8,128)(2,1)S(1)} %get-tuple-element.135.own_ref), channel_id=1, source_target_pairs={{0,64},{32,96},{64,0},{96,32},{1,65},{33,97},{65,1},{97,33},{2,66}... | collective-permute-start | bytes 12296 | tf_op jit(solution)/shard_map/ppermute | solution.py:613
  144.9 14.7 %copy-start.54 = (bf16[128,64]{1,0:T(8,128)(2,1)S(1)}, bf16[128,64]{1,0:T(8,128)(2,1)}, u32[]{:S(2)}) copy-start(bf16[128,64]{1,0:T(8,128)(2,1)} %copy.30) | copy-start | bytes 49156
  144.9 18.7 %copy-start.15 = (f32[14,448,128]{2,1,0:T(8,128)S(1)}, f32[14,448,128]{2,1,0:T(8,128)}, u32[]{:S(2)}) copy-start(f32[14,448,128]{2,1,0:T(8,128)} %copy-done.14) | copy-start | bytes 9633796
  144.9 18.7 %copy-start.26 = (bf16[14,448,128]{2,1,0:T(8,128)(2,1)S(1)}, bf16[14,448,128]{2,1,0:T(8,128)(2,1)}, u32[]{:S(2)}) copy-start(bf16[14,448,128]{2,1,0:T(8,128)(2,1)} %copy-done.25) | copy-start | bytes 4816900
  156.9 4.7 %collective-permute-start.23 = (bf16[16,128]{1,0:T(8,128)(2,1)S(1)}, bf16[16,128]{1,0:T(8,128)(2,1)S(1)}, u32[]{:S(2)}, u32[]{:S(2)}) collective-permute-start(bf16[16,128]{1,0:T(8,128)(2,1)S(1)} %get-tuple-element.138.own_ref), channel_id=1, source_target_pairs={{0,32},{32,64},{64,96},{96,0},{1,33},{33,65},{65,97},{97,1},{2,34}... | collective-permute-start | bytes 12296 | tf_op jit(solution)/shard_map/ppermute | solution.py:613
  156.9 4.7 %collective-permute-start.24 = (bf16[16,128]{1,0:T(8,128)(2,1)S(1)}, bf16[16,128]{1,0:T(8,128)(2,1)S(1)}, u32[]{:S(2)}, u32[]{:S(2)}) collective-permute-start(bf16[16,128]{1,0:T(8,128)(2,1)S(1)} %get-tuple-element.138.own_ref), channel_id=1, source_target_pairs={{0,96},{32,0},{64,32},{96,64},{1,97},{33,1},{65,33},{97,65},{2,98}... | collective-permute-start | bytes 12296 | tf_op jit(solution)/shard_map/ppermute | solution.py:613
  159.6 4.0 %collective-permute-start.25 = (bf16[16,128]{1,0:T(8,128)(2,1)S(1)}, bf16[16,128]{1,0:T(8,128)(2,1)S(1)}, u32[]{:S(2)}, u32[]{:S(2)}) collective-permute-start(bf16[16,128]{1,0:T(8,128)(2,1)S(1)} %get-tuple-element.138.own_ref), channel_id=1, source_target_pairs={{0,64},{32,96},{64,0},{96,32},{1,65},{33,97},{65,1},{97,33},{2,66}... | collective-permute-start | bytes 12296 | tf_op jit(solution)/shard_map/ppermute | solution.py:613
  171.5 48.0 %all-to-all-start.1 = ((bf16[128,56,128]{2,1,0:T(8,128)(2,1)}), bf16[128,56,128]{2,1,0:T(8,128)(2,1)S(1)}, u32[]{:S(2)}, u32[]{:S(2)}) async-start(bf16[128,56,128]{2,1,0:T(8,128)(2,1)} %copy-done.24), calls=%async_computation.1 | async-start | bytes 3670016 | tf_op jit(solution)/shard_map/all_to_all | solution.py:750
  219.5 10.3 %copy-start.49 = (bf16[128,56]{0,1:T(8,128)(2,1)S(1)}, bf16[128,56]{0,1:T(8,128)(2,1)}, u32[]{:S(2)}) copy-start(bf16[128,56]{0,1:T(8,128)(2,1)} %param.12) | copy-start | bytes 43012
  219.5 31.9 %all-to-all-start.2 = ((bf16[128,40,128]{2,1,0:T(8,128)(2,1)}), bf16[128,40,128]{2,1,0:T(8,128)(2,1)}, u32[]{:S(2)}, u32[]{:S(2)}) async-start(bf16[128,40,128]{2,1,0:T(8,128)(2,1)} %maximum_maximum_fusion), calls=%async_computation.2 | async-start | bytes 2621440 | tf_op jit(solution)/shard_map/all_to_all | solution.py:770
  253.7 14.1 %all-to-all-start.3 = ((bf16[128,1,128]{2,1,0:T(2,128)(2,1)}), bf16[128,1,128]{2,1,0:T(2,128)(2,1)S(1)}, u32[]{:S(2)}, u32[]{:S(2)}) async-start(bf16[128,1,128]{2,1,0:T(2,128)(2,1)} %copy.33), calls=%async_computation.3 | async-start | bytes 131072 | tf_op jit(solution)/shard_map/all_to_all | solution.py:778
  (39 other events, 92.1 us)
